TPU v7x, 32 devices: a whole 2x2x4 slice. The times are simulated.
32 devices in a mesh: dp: 4 (over y, core), ctx: 8 (over z, x).
Axes of the slice: x: 2, y: 2, z: 4, core: 2. Of those that a mesh axis runs over, the one named last changes fastest.
Arguments:
- tokens: bfloat16 [4096, 768], P(('dp', 'ctx')), may hold values from -15 to 15
- w_query: bfloat16 [768, 768], P(('dp', 'ctx')), may hold values from -0.21875 to 0.21875
- w_key: bfloat16 [768, 768], P(('dp', 'ctx')), may hold values from -0.21875 to 0.21875
- w_value: bfloat16 [768, 768], P(('dp', 'ctx')), may hold values from -0.21875 to 0.21875
- w_out: bfloat16 [768, 768], P(('dp', 'ctx')), may hold values from -0.4375 to 0.4375
- b_query: bfloat16 [768], P(('dp', 'ctx')), may hold values from -3 to 3
- b_value: bfloat16 [768], P(('dp', 'ctx')), may hold values from -1.1953125 to 1.1953125
- b_out: bfloat16 [768], P(('dp', 'ctx')), may hold values from -3 to 3
- norm1_gain: bfloat16 [768], P(('dp', 'ctx')), may hold values from 0.099609375 to 1.8984375
- norm1_shift: bfloat16 [768], P(('dp', 'ctx')), may hold values from -3 to 3
- w_in: bfloat16 [768, 3072], P(('dp', 'ctx')), may hold values from -0.21875 to 0.21875
- b_in: bfloat16 [3072], P(('dp', 'ctx')), may hold values from -3 to 3
- w_back: bfloat16 [3072, 768], P(('dp', 'ctx')), may hold values from -0.109375 to 0.109375
- b_back: bfloat16 [768], P(('dp', 'ctx')), may hold values from -3 to 3
- norm2_gain: bfloat16 [768], P(('dp', 'ctx')), may hold values from 0.099609375 to 1.8984375
- norm2_shift: bfloat16 [768], P(('dp', 'ctx')), may hold values from -3 to 3
- cotangent: bfloat16 [4096, 768], P(('dp', 'ctx')), may hold values from -6 to 6
Outputs:
- layer_out: bfloat16 [4096, 768], P(('dp', 'ctx'))
- input_grad: float32 [4096, 768], P(('dp', 'ctx'))
- w_query_grad: float32 [768, 768], P(('dp', 'ctx'))
- w_key_grad: float32 [768, 768], P(('dp', 'ctx'))
- w_value_grad: float32 [768, 768], P(('dp', 'ctx'))
- w_out_grad: float32 [768, 768], P(('dp', 'ctx'))
- b_query_grad: float32 [768], P(('dp', 'ctx'))
- b_value_grad: float32 [768], P(('dp', 'ctx'))
- b_out_grad: float32 [768], P(('dp', 'ctx'))
- norm1_gain_grad: float32 [768], P(('dp', 'ctx'))
- norm1_shift_grad: float32 [768], P(('dp', 'ctx'))
- w_in_grad: float32 [768, 3072], P(('dp', 'ctx'))
- b_in_grad: float32 [3072], P(('dp', 'ctx'))
- w_back_grad: float32 [3072, 768], P(('dp', 'ctx'))
- b_back_grad: float32 [768], P(('dp', 'ctx'))
- norm2_gain_grad: float32 [768], P(('dp', 'ctx'))
- norm2_shift_grad: float32 [768], P(('dp', 'ctx'))
- rms_values: float32 [2], replicated
All inputs are finite; a program needn't handle non-finite values.
Results may differ from a plain program's by a relative error of at most 0.015.
Values may be sent and summed in bfloat16 or wider, within the bound.
A program may use at most 256 MiB of HBM per device.

v0:
```python
from functools import partial

import jax
import jax.numpy as jnp
from jax import lax
from jax.sharding import PartitionSpec as P

DH = 64


epsilon = 1e-12


def normalize(values, gain, shift):
    average = jnp.mean(values, axis=-1, keepdims=True)
    centered = values - average
    spread = jnp.mean(centered * centered, axis=-1, keepdims=True)
    inverse = lax.rsqrt(spread + epsilon)
    scaled = centered * inverse
    return (scaled * gain + shift, scaled, inverse)


def normalize_back(incoming, scaled, inverse, gain):
    along = incoming * gain
    inner = (
        along
        - jnp.mean(along, axis=-1, keepdims=True)
        - scaled * jnp.mean(along * scaled, axis=-1, keepdims=True)
    )
    return (inverse * inner, jnp.sum(incoming * scaled, axis=0), jnp.sum(incoming, axis=0))


def split_heads(row_array):
    return row_array.reshape(row_array.shape[0], -1, DH)


def local(
    tokens,
    w_query,
    w_key,
    w_value,
    w_out,
    b_query,
    b_value,
    b_out,
    norm1_gain,
    norm1_shift,
    w_in,
    b_in,
    w_back,
    b_back,
    norm2_gain,
    norm2_shift,
    cotangent,
):
    f32 = jnp.float32
    bf16 = jnp.bfloat16
    attn_parts = (
        lax.all_gather(w_query, ("dp", "ctx"), axis=0, tiled=True),
        lax.all_gather(w_key, ("dp", "ctx"), axis=0, tiled=True),
        lax.all_gather(w_value, ("dp", "ctx"), axis=0, tiled=True),
        lax.all_gather(w_out, ("dp", "ctx"), axis=0, tiled=True),
        lax.all_gather(b_query, ("dp", "ctx"), axis=0, tiled=True),
        lax.all_gather(b_value, ("dp", "ctx"), axis=0, tiled=True),
        lax.all_gather(b_out, ("dp", "ctx"), axis=0, tiled=True),
        lax.all_gather(norm1_gain, ("dp", "ctx"), axis=0, tiled=True),
        lax.all_gather(norm1_shift, ("dp", "ctx"), axis=0, tiled=True),
    )
    wq_full, wk_full, wv_full, wo_full, bq_full, bv_full, bo_full, gain_one, shift_one = attn_parts
    row_count = tokens.shape[0]
    model_width = tokens.shape[1]
    residual = tokens.astype(f32)
    query_rows = (
        jnp.dot(tokens, wq_full, preferred_element_type=f32) + bq_full.astype(f32)
    ).astype(bf16)
    key_rows = jnp.dot(tokens, wk_full, preferred_element_type=f32).astype(bf16)
    value_rows = (
        jnp.dot(tokens, wv_full, preferred_element_type=f32) + bv_full.astype(f32)
    ).astype(bf16)
    query_heads = split_heads(query_rows)
    key_local = split_heads(key_rows)
    value_local = split_heads(value_rows)
    portion = (
        lax.all_gather(key_rows, "ctx", axis=0, tiled=True),
        lax.all_gather(value_rows, "ctx", axis=0, tiled=True),
    )
    key_heads = split_heads(portion[0])
    value_heads = split_heads(portion[1])
    scores = jnp.einsum("qhd,khd->hqk", query_heads, key_heads, preferred_element_type=f32) * 0.125
    weights = jnp.exp(scores)
    summed = jnp.einsum(
        "hqk,khd->qhd", weights.astype(bf16), value_heads, preferred_element_type=f32
    )
    summed_all = summed.reshape(row_count, model_width)
    totals = jnp.sum(weights, axis=-1)
    totals_rows = jnp.transpose(totals)
    mixed_heads = split_heads(summed_all) / totals_rows[:, :, None]
    mixed = mixed_heads.reshape(row_count, model_width)
    mixed_low = mixed.astype(bf16)
    branch_attn = jnp.dot(mixed_low, wo_full, preferred_element_type=f32) + bo_full.astype(f32)
    gain_one32 = gain_one.astype(f32)
    stream_one = residual + branch_attn
    hidden, scaled_one, inverse_one = normalize(stream_one, gain_one32, shift_one.astype(f32))
    ffn_parts = (
        lax.all_gather(w_in, ("dp", "ctx"), axis=0, tiled=True),
        lax.all_gather(w_back, ("dp", "ctx"), axis=0, tiled=True),
        lax.all_gather(b_in, ("dp", "ctx"), axis=0, tiled=True),
        lax.all_gather(b_back, ("dp", "ctx"), axis=0, tiled=True),
        lax.all_gather(norm2_gain, ("dp", "ctx"), axis=0, tiled=True),
        lax.all_gather(norm2_shift, ("dp", "ctx"), axis=0, tiled=True),
    )
    w1_full, w2_full, b1_full, b2_full, gain_two, shift_two = ffn_parts
    hidden_low = hidden.astype(bf16)
    pre_act = jnp.dot(hidden_low, w1_full, preferred_element_type=f32) + b1_full.astype(f32)
    activated, gelu_pull = jax.vjp(partial(jax.nn.gelu, approximate=False), pre_act)
    act_low = activated.astype(bf16)
    branch_ffn = jnp.dot(act_low, w2_full, preferred_element_type=f32) + b2_full.astype(f32)
    gain_two32 = gain_two.astype(f32)
    normed_out, scaled_two, inverse_two = normalize(
        hidden + branch_ffn, gain_two32, shift_two.astype(f32)
    )
    layer_out = normed_out.astype(bf16)
    square_sums = lax.psum(
        (jnp.sum(residual * residual), jnp.sum(stream_one * stream_one)), ("dp", "ctx")
    )
    entries = row_count * model_width * lax.axis_size("dp") * lax.axis_size("ctx")
    rms_values = jnp.sqrt(jnp.stack(square_sums) / entries)
    upstream = cotangent.astype(f32)
    dsum_two, gain_two_grad, shift_two_grad = normalize_back(
        upstream, scaled_two, inverse_two, gain_two32
    )
    ffn_grad = dsum_two.astype(bf16)
    b2_grad = jnp.sum(ffn_grad, axis=0, dtype=f32)
    w2_grad = jnp.einsum("tf,td->fd", act_low, ffn_grad, preferred_element_type=f32)
    act_grad = jnp.einsum("td,fd->tf", ffn_grad, w2_full, preferred_element_type=f32)
    pre_grad = gelu_pull(act_grad)[0].astype(bf16)
    b1_grad = jnp.sum(pre_grad, axis=0, dtype=f32)
    w1_grad = jnp.einsum("td,tf->df", hidden_low, pre_grad, preferred_element_type=f32)
    hidden_grad = dsum_two + jnp.einsum("tf,df->td", pre_grad, w1_full, preferred_element_type=f32)
    dsum_one, gain_one_grad, shift_one_grad = normalize_back(
        hidden_grad, scaled_one, inverse_one, gain_one32
    )
    attn_grad = dsum_one.astype(bf16)
    bo_grad = jnp.sum(attn_grad, axis=0, dtype=f32)
    wo_grad = jnp.einsum("te,td->ed", mixed_low, attn_grad, preferred_element_type=f32)
    mixed_grad = split_heads(
        jnp.einsum("td,ed->te", attn_grad, wo_full, preferred_element_type=f32)
    )
    grad_heads = (mixed_grad / totals_rows[:, :, None]).astype(bf16)
    delta_rows = jnp.sum(mixed_grad * mixed_heads, axis=-1) / totals_rows
    delta_heads = jnp.transpose(delta_rows)
    grad_rows = grad_heads.reshape(row_count, model_width)
    portion = (
        lax.all_gather(key_rows, "ctx", axis=0, tiled=True),
        lax.all_gather(value_rows, "ctx", axis=0, tiled=True),
    )
    key_heads = split_heads(portion[0])
    value_heads = split_heads(portion[1])
    scores = jnp.einsum("qhd,khd->hqk", query_heads, key_heads, preferred_element_type=f32) * 0.125
    weights = jnp.exp(scores)
    across = jnp.einsum("qhd,khd->hqk", grad_heads, value_heads, preferred_element_type=f32)
    slopes = (weights * (across - delta_heads[:, :, None])).astype(bf16)
    part_grad = jnp.einsum("hqk,khd->qhd", slopes, key_heads, preferred_element_type=f32)
    query_acc = part_grad.reshape(row_count, model_width)
    delta_all = lax.all_gather(delta_rows, "ctx", axis=0, tiled=True)
    portion = (
        lax.all_gather(query_rows, "ctx", axis=0, tiled=True),
        lax.all_gather(grad_rows, "ctx", axis=0, tiled=True),
    )
    query_part = split_heads(portion[0])
    grad_part = split_heads(portion[1])
    scores = jnp.einsum("qhd,khd->hqk", query_part, key_local, preferred_element_type=f32) * 0.125
    weights = jnp.exp(scores)
    value_part = jnp.einsum(
        "hqk,qhd->khd", weights.astype(bf16), grad_part, preferred_element_type=f32
    )
    across = jnp.einsum("qhd,khd->hqk", grad_part, value_local, preferred_element_type=f32)
    slopes = (weights * (across - jnp.transpose(delta_all)[:, :, None])).astype(bf16)
    key_part = jnp.einsum("hqk,qhd->khd", slopes, query_part, preferred_element_type=f32)
    key_acc = key_part.reshape(row_count, model_width)
    value_acc = value_part.reshape(row_count, model_width)
    query_grad = (0.125 * query_acc).astype(bf16)
    key_grad = (0.125 * key_acc).astype(bf16)
    value_grad = value_acc.astype(bf16)
    wq_grad = jnp.einsum("td,te->de", tokens, query_grad, preferred_element_type=f32)
    wk_grad = jnp.einsum("td,te->de", tokens, key_grad, preferred_element_type=f32)
    wv_grad = jnp.einsum("td,te->de", tokens, value_grad, preferred_element_type=f32)
    bq_grad = jnp.sum(query_grad, axis=0, dtype=f32)
    bv_grad = jnp.sum(value_grad, axis=0, dtype=f32)
    input_grad = (
        dsum_one
        + jnp.einsum("te,de->td", query_grad, wq_full, preferred_element_type=f32)
        + jnp.einsum("te,de->td", key_grad, wk_full, preferred_element_type=f32)
        + jnp.einsum("te,de->td", value_grad, wv_full, preferred_element_type=f32)
    )
    attn_owned = (
        lax.psum_scatter(wq_grad, ("dp", "ctx"), scatter_dimension=0, tiled=True),
        lax.psum_scatter(wk_grad, ("dp", "ctx"), scatter_dimension=0, tiled=True),
        lax.psum_scatter(wv_grad, ("dp", "ctx"), scatter_dimension=0, tiled=True),
        lax.psum_scatter(wo_grad, ("dp", "ctx"), scatter_dimension=0, tiled=True),
        lax.psum_scatter(bq_grad, ("dp", "ctx"), scatter_dimension=0, tiled=True),
        lax.psum_scatter(bv_grad, ("dp", "ctx"), scatter_dimension=0, tiled=True),
        lax.psum_scatter(bo_grad, ("dp", "ctx"), scatter_dimension=0, tiled=True),
        lax.psum_scatter(gain_one_grad, ("dp", "ctx"), scatter_dimension=0, tiled=True),
        lax.psum_scatter(shift_one_grad, ("dp", "ctx"), scatter_dimension=0, tiled=True),
    )
    ffn_owned = (
        lax.psum_scatter(w1_grad, ("dp", "ctx"), scatter_dimension=0, tiled=True),
        lax.psum_scatter(b1_grad, ("dp", "ctx"), scatter_dimension=0, tiled=True),
        lax.psum_scatter(w2_grad, ("dp", "ctx"), scatter_dimension=0, tiled=True),
        lax.psum_scatter(b2_grad, ("dp", "ctx"), scatter_dimension=0, tiled=True),
        lax.psum_scatter(gain_two_grad, ("dp", "ctx"), scatter_dimension=0, tiled=True),
        lax.psum_scatter(shift_two_grad, ("dp", "ctx"), scatter_dimension=0, tiled=True),
    )
    return (
        layer_out,
        input_grad,
        attn_owned[0],
        attn_owned[1],
        attn_owned[2],
        attn_owned[3],
        attn_owned[4],
        attn_owned[5],
        attn_owned[6],
        attn_owned[7],
        attn_owned[8],
        ffn_owned[0],
        ffn_owned[1],
        ffn_owned[2],
        ffn_owned[3],
        ffn_owned[4],
        ffn_owned[5],
        rms_values,
    )


def solution(mesh):
    in_specs = (
        P(("dp", "ctx"), None),
        P(("dp", "ctx"), None),
        P(("dp", "ctx"), None),
        P(("dp", "ctx"), None),
        P(("dp", "ctx"), None),
        P(("dp", "ctx")),
        P(("dp", "ctx")),
        P(("dp", "ctx")),
        P(("dp", "ctx")),
        P(("dp", "ctx")),
        P(("dp", "ctx"), None),
        P(("dp", "ctx")),
        P(("dp", "ctx"), None),
        P(("dp", "ctx")),
        P(("dp", "ctx")),
        P(("dp", "ctx")),
        P(("dp", "ctx"), None),
    )
    out_specs = (
        P(("dp", "ctx"), None),
        P(("dp", "ctx"), None),
        P(("dp", "ctx"), None),
        P(("dp", "ctx"), None),
        P(("dp", "ctx"), None),
        P(("dp", "ctx"), None),
        P(("dp", "ctx")),
        P(("dp", "ctx")),
        P(("dp", "ctx")),
        P(("dp", "ctx")),
        P(("dp", "ctx")),
        P(("dp", "ctx"), None),
        P(("dp", "ctx")),
        P(("dp", "ctx"), None),
        P(("dp", "ctx")),
        P(("dp", "ctx")),
        P(("dp", "ctx")),
        P(),
    )
    return jax.shard_map(local, mesh=mesh, in_specs=in_specs, out_specs=out_specs, check_vma=False)
```

profile of v0, /device:TPU:1, one launch (start us, length us, event | category | flops | bytes accessed | tf_op | source)
XLA Modules:
  0.0 1253.1 jit_solution(6676247992770424613)
XLA Ops:
  9.6 58.3 %all-gather.17.cloned.1.call-done = bf16[768,768]{1,0:T(8,128)(2,1)} async-done(((bf16[24,768]{1,0:T(8,128)(2,1)}), bf16[768,768]{1,0:T(8,128)(2,1)}) %all-gather.17.cloned.1.call-update) | async-done | bytes 1179664 | tf_op jit(solution)/shard_map/all_gather | solution.py:60
  67.8 2.4 convolution_convert_fusion
  72.5 38.4 %all-reduce.19 = (bf16[3072]{0:T(1024)(128)(2,1)S(1)}, bf16[768]{0:T(1024)(128)(2,1)S(1)}, bf16[768]{0:T(1024)(128)(2,1)S(1)}, bf16[768]{0:T(1024)(128)(2,1)S(1)...) all-reduce(bf16[3072]{0:T(1024)(128)(2,1)S(1)} %dynamic-update-slic, ...), channel_id=1, replica_groups=mesh['dp'=4,'ctx'=8] {'dp','ctx'}, use_global_device_ids=true, to_apply=%add.5 | all-reduce | flops 9216 | bytes 36864
  110.9 13.1 %all-gather.11.cloned.1.call-done = bf16[768,768]{1,0:T(8,128)(2,1)} async-done(((bf16[24,768]{1,0:T(8,128)(2,1)}), bf16[768,768]{1,0:T(8,128)(2,1)}) %all-gather.11.cloned.1.call-update) | async-done | bytes 1179664 | tf_op jit(solution)/shard_map/all_gather | solution.py:61
  128.5 51.5 %all-gather.15.cloned.1.call-done = bf16[768,768]{1,0:T(8,128)(2,1)} async-done(((bf16[24,768]{1,0:T(8,128)(2,1)}), bf16[768,768]{1,0:T(8,128)(2,1)}) %all-gather.15.cloned.1.call-update) | async-done | bytes 1179664 | tf_op jit(solution)/shard_map/all_gather | solution.py:59
  182.6 42.2 %all-gather.19.cloned.1.call-done = bf16[1024,768]{1,0:T(8,128)(2,1)} async-done(((bf16[128,768]{1,0:T(8,128)(2,1)}), bf16[1024,768]{1,0:T(8,128)(2,1)}) %all-gather.19.cloned.1.call-update) | async-done | bytes 1572880 | tf_op jit(solution)/shard_map/all_gather | solution.py:84
  226.5 3.8 fusion.1
  230.3 40.1 %all-gather.13.cloned.1.call-done = bf16[1024,768]{1,0:T(8,128)(2,1)} async-done(((bf16[128,768]{1,0:T(8,128)(2,1)}), bf16[1024,768]{1,0:T(8,128)(2,1)}) %all-gather.13.cloned.1.call-update) | async-done | bytes 1572880 | tf_op jit(solution)/shard_map/all_gather | solution.py:85
  272.1 4.8 fusion.69
  276.9 50.4 %all-gather.21.cloned.1.call-done = bf16[768,768]{1,0:T(8,128)(2,1)} async-done(((bf16[24,768]{1,0:T(8,128)(2,1)}), bf16[768,768]{1,0:T(8,128)(2,1)}) %all-gather.21.cloned.1.call-update) | async-done | bytes 1179664 | tf_op jit(solution)/shard_map/all_gather | solution.py:62
  330.2 62.7 %all-gather.23.cloned.1.call-done = bf16[768,3072]{1,0:T(8,128)(2,1)} async-done(((bf16[24,3072]{1,0:T(8,128)(2,1)}), bf16[768,3072]{1,0:T(8,128)(2,1)}) %all-gather.23.cloned.1.call-update) | async-done | bytes 4718608 | tf_op jit(solution)/shard_map/all_gather | solution.py:105
  392.9 8.4 multiply_convert_fusion.4
  401.4 57.1 %all-gather.25.cloned.1.call-done = bf16[3072,768]{1,0:T(8,128)(2,1)} async-done(((bf16[96,768]{1,0:T(8,128)(2,1)}), bf16[3072,768]{1,0:T(8,128)(2,1)}) %all-gather.25.cloned.1.call-update) | async-done | bytes 4718608 | tf_op jit(solution)/shard_map/all_gather | solution.py:106
  458.5 3.4 fusion.71
  464.4 2.5 convert_reduce_fusion
  466.9 2.5 multiply_reduce_fusion.1
  476.9 6.5 convert_reduce_fusion.5
  487.1 15.5 %all-gather.27.cloned.1.call-done = bf16[1024,768]{1,0:T(8,128)(2,1)} async-done(((bf16[128,768]{1,0:T(8,128)(2,1)}), bf16[1024,768]{1,0:T(8,128)(2,1)}) %all-gather.27.cloned.1.call-update) | async-done | bytes 1572880 | tf_op jit(solution)/shard_map/all_gather | solution.py:167
  504.4 3.7 fusion.72
  508.1 24.5 %all_gather.81 = f32[1024,12]{0,1:T(8,128)S(1)} all-gather(f32[128,12]{0,1:T(8,128)S(1)} %bitcast_divide_fusion.1), channel_id=1, replica_groups=mesh['dp'=4,'ctx'=8] {'ctx'}, dimensions={0}, use_global_device_ids=true | all-gather | bytes 55296 | tf_op jit(solution)/shard_map/all_gather | solution.py:165
  532.6 15.3 %all-gather.29.cloned.1.call-done = bf16[1024,768]{1,0:T(8,128)(2,1)} async-done(((bf16[128,768]{1,0:T(8,128)(2,1)}), bf16[1024,768]{1,0:T(8,128)(2,1)}) %all-gather.29.cloned.1.call-update) | async-done | bytes 1572880 | tf_op jit(solution)/shard_map/all_gather | solution.py:168
  549.6 6.7 fusion.28
  560.2 4.2 convert_reduce_fusion.4
  568.0 5.2 fusion.64
  574.5 5.0 fusion.54
  582.4 41.3 %all-reduce.18 = (f32[768]{0:T(1024)S(1)}, f32[768]{0:T(1024)S(1)}, f32[768]{0:T(1024)S(1)}, f32[768]{0:T(1024)S(1)}, f32[768]{0:T(1024)S(1)}, /*index=5*/f32[30...) all-reduce(f32[768]{0:T(1024)S(1)} %reduce_sum.207, ...), channel_id=6, replica_groups=mesh['dp'=4,'ctx'=8] {'dp','ctx'}, use_global_device_ids=true, to_apply=%region_15.0.clone | all-reduce | flops 9218 | bytes 73744
  633.5 17.3 %reduce-scatter.13.cloned.1.call-done = f32[24,768]{1,0:T(8,128)} async-done(((f32[768,768]{1,0:T(8,128)}), f32[24,768]{1,0:T(8,128)}) %reduce-scatter.13.cloned.1.call-update) | async-done | bytes 73744 | tf_op jit(solution)/shard_map/reduce_scatter | solution.py:200
  650.8 104.6 %reduce-scatter.19.cloned.1.call-done = f32[24,768]{1,0:T(8,128)} async-done(((f32[768,768]{1,0:T(8,128)}), f32[24,768]{1,0:T(8,128)}) %reduce-scatter.19.cloned.1.call-update) | async-done | bytes 73744
  755.4 104.0 %reduce-scatter.21.cloned.1.call-done = f32[24,768]{1,0:T(8,128)} async-done(((f32[768,768]{1,0:T(8,128)}), f32[24,768]{1,0:T(8,128)}) %reduce-scatter.21.cloned.1.call-update) | async-done | bytes 73744
  859.4 104.6 %reduce-scatter.23.cloned.1.call-done = f32[24,768]{1,0:T(8,128)} async-done(((f32[768,768]{1,0:T(8,128)}), f32[24,768]{1,0:T(8,128)}) %reduce-scatter.23.cloned.1.call-update) | async-done | bytes 73744
  964.0 140.6 %reduce-scatter.15.cloned.1.call-done = f32[24,3072]{1,0:T(8,128)} async-done(((f32[768,3072]{1,0:T(8,128)}), f32[24,3072]{1,0:T(8,128)}) %reduce-scatter.15.cloned.1.call-update) | async-done | bytes 294928 | tf_op jit(solution)/shard_map/reduce_scatter | solution.py:208
  1104.6 142.0 %reduce-scatter.17.cloned.1.call-done = f32[96,768]{1,0:T(8,128)} async-done(((f32[3072,768]{1,0:T(8,128)}), f32[96,768]{1,0:T(8,128)}) %reduce-scatter.17.cloned.1.call-update) | async-done | bytes 294928 | tf_op jit(solution)/shard_map/reduce_scatter | solution.py:210
  (207 shorter events, 55.9 us)
Async XLA Ops:
  7.2 116.8 %copy-start = (bf16[128,768]{1,0:T(8,128)(2,1)S(1)}, bf16[128,768]{1,0:T(8,128)(2,1)}, u32[]{:S(2)}) copy-start(bf16[128,768]{1,0:T(8,128)(2,1)} %param.17) | copy-start | bytes 589828
  7.2 63.1 %copy-start.32 = (bf16[24]{0:T(256)(128)(2,1)S(1)}, bf16[24]{0:T(256)(128)(2,1)}, u32[]{:S(2)}) copy-start(bf16[24]{0:T(256)(128)(2,1)} %param.23) | copy-start | bytes 148
  7.2 63.3 %copy-start.33 = (bf16[24]{0:T(256)(128)(2,1)S(1)}, bf16[24]{0:T(256)(128)(2,1)}, u32[]{:S(2)}) copy-start(bf16[24]{0:T(256)(128)(2,1)} %param.22) | copy-start | bytes 148
  7.2 63.6 %copy-start.34 = (bf16[24]{0:T(256)(128)(2,1)S(1)}, bf16[24]{0:T(256)(128)(2,1)}, u32[]{:S(2)}) copy-start(bf16[24]{0:T(256)(128)(2,1)} %param.24) | copy-start | bytes 148
  7.2 63.8 %copy-start.35 = (bf16[24]{0:T(256)(128)(2,1)S(1)}, bf16[24]{0:T(256)(128)(2,1)}, u32[]{:S(2)}) copy-start(bf16[24]{0:T(256)(128)(2,1)} %param.25) | copy-start | bytes 148
  7.2 64.0 %copy-start.36 = (bf16[24]{0:T(256)(128)(2,1)S(1)}, bf16[24]{0:T(256)(128)(2,1)}, u32[]{:S(2)}) copy-start(bf16[24]{0:T(256)(128)(2,1)} %param.26) | copy-start | bytes 148
  7.3 64.2 %copy-start.37 = (bf16[24]{0:T(256)(128)(2,1)S(1)}, bf16[24]{0:T(256)(128)(2,1)}, u32[]{:S(2)}) copy-start(bf16[24]{0:T(256)(128)(2,1)} %param.30) | copy-start | bytes 148
  7.3 64.5 %copy-start.38 = (bf16[24]{0:T(256)(128)(2,1)S(1)}, bf16[24]{0:T(256)(128)(2,1)}, u32[]{:S(2)}) copy-start(bf16[24]{0:T(256)(128)(2,1)} %param.31) | copy-start | bytes 148
  7.3 64.7 %copy-start.39 = (bf16[24]{0:T(256)(128)(2,1)S(1)}, bf16[24]{0:T(256)(128)(2,1)}, u32[]{:S(2)}) copy-start(bf16[24]{0:T(256)(128)(2,1)} %param.32) | copy-start | bytes 148
  7.3 64.9 %copy-start.40 = (bf16[96]{0:T(256)(128)(2,1)S(1)}, bf16[96]{0:T(256)(128)(2,1)}, u32[]{:S(2)}) copy-start(bf16[96]{0:T(256)(128)(2,1)} %param.28) | copy-start | bytes 580
  7.3 60.5 %all-gather.17.cloned.1.call-start = ((), (), s32[]{:S(2)}) async-start(), calls=%async_computation.9 | async-start | bytes 1216512 | tf_op jit(solution)/shard_map/all_gather | solution.py:60
  8.0 116.0 %all-gather.11.cloned.1.call-start = ((), (), s32[]{:S(2)}) async-start(), calls=%async_computation.6 | async-start | bytes 1216512 | tf_op jit(solution)/shard_map/all_gather | solution.py:61
  8.8 171.3 %all-gather.15.cloned.1.call-start = ((), (), s32[]{:S(2)}) async-start(), calls=%async_computation.8 | async-start | bytes 1216512 | tf_op jit(solution)/shard_map/all_gather | solution.py:59
  9.5 215.3 %all-gather.19.cloned.1.call-start = ((), (), s32[]{:S(2)}) async-start(), calls=%async_computation.10 | async-start | bytes 1769472 | tf_op jit(solution)/shard_map/all_gather | solution.py:84
  70.2 200.2 %all-gather.13.cloned.1.call-start = ((), (), s32[]{:S(2)}) async-start(), calls=%async_computation.7 | async-start | bytes 1769472 | tf_op jit(solution)/shard_map/all_gather | solution.py:85
  126.3 201.0 %all-gather.21.cloned.1.call-start = ((), (), s32[]{:S(2)}) async-start(), calls=%async_computation.11 | async-start | bytes 1216512 | tf_op jit(solution)/shard_map/all_gather | solution.py:62
  126.9 266.0 %all-gather.23.cloned.1.call-start = ((), (), s32[]{:S(2)}) async-start(), calls=%async_computation.12 | async-start | bytes 4866048 | tf_op jit(solution)/shard_map/all_gather | solution.py:105
  127.7 330.8 %all-gather.25.cloned.1.call-start = ((), (), s32[]{:S(2)}) async-start(), calls=%async_computation.13 | async-start | bytes 4866048 | tf_op jit(solution)/shard_map/all_gather | solution.py:106
  128.4 374.2 %all-gather.27.cloned.1.call-start = ((), (), s32[]{:S(2)}) async-start(), calls=%async_computation.14 | async-start | bytes 1769472 | tf_op jit(solution)/shard_map/all_gather | solution.py:167
  182.4 365.5 %all-gather.29.cloned.1.call-start = ((), (), s32[]{:S(2)}) async-start(), calls=%async_computation.15 | async-start | bytes 1769472 | tf_op jit(solution)/shard_map/all_gather | solution.py:168
  329.0 137.8 %copy-start.25 = (f32[128]{0:T(128)}, f32[128]{0:T(128)S(1)}, u32[]{:S(2)}) copy-start(f32[128]{0:T(128)S(1)} %broadcast_multiply_fusion.5) | copy-start | bytes 1540
  329.3 137.6 %copy-start.29 = (f32[128]{0:T(128)}, f32[128]{0:T(128)S(1)}, u32[]{:S(2)}) copy-start(f32[128]{0:T(128)S(1)} %add_rsqrt_fusion.1) | copy-start | bytes 1540
  401.4 60.5 %copy-start.9 = (bf16[128,3072]{1,0:T(8,128)(2,1)}, bf16[128,3072]{1,0:T(8,128)(2,1)S(1)}, u32[]{:S(2)}) copy-start(bf16[128,3072]{1,0:T(8,128)(2,1)S(1)} %get-tuple-element.105) | copy-start | bytes 2359300
  472.1 178.8 %reduce-scatter.13.cloned.1.call-start = ((), (), s32[]{:S(2)}) async-start(), calls=%async_computation.16 | async-start | bytes 2433024 | tf_op jit(solution)/shard_map/reduce_scatter | solution.py:200
  474.0 281.4 %reduce-scatter.19.cloned.1.call-start = ((), (), s32[]{:S(2)}) async-start(), calls=%async_computation.19 | async-start | bytes 2433024
  485.9 373.5 %reduce-scatter.21.cloned.1.call-start = ((), (), s32[]{:S(2)}) async-start(), calls=%async_computation.20 | async-start | bytes 2433024
  549.6 6.7 copy-start.2
  558.8 405.2 %reduce-scatter.23.cloned.1.call-start = ((), (), s32[]{:S(2)}) async-start(), calls=%async_computation.21 | async-start | bytes 2433024
  566.9 537.7 %reduce-scatter.15.cloned.1.call-start = ((), (), s32[]{:S(2)}) async-start(), calls=%async_computation.17 | async-start | bytes 9732096 | tf_op jit(solution)/shard_map/reduce_scatter | solution.py:208
  573.2 673.3 %reduce-scatter.17.cloned.1.call-start = ((), (), s32[]{:S(2)}) async-start(), calls=%async_computation.18 | async-start | bytes 9732096 | tf_op jit(solution)/shard_map/reduce_scatter | solution.py:210
  579.5 51.2 %copy-start.6 = (bf16[768,768]{1,0:T(8,128)(2,1)S(1)}, bf16[768,768]{1,0:T(8,128)(2,1)}, u32[]{:S(2)}) copy-start(bf16[768,768]{1,0:T(8,128)(2,1)} %all-gather.17.cloned.1.call-done) | copy-start | bytes 3538948
  582.3 49.9 %copy-start.7 = (bf16[768,768]{1,0:T(8,128)(2,1)S(1)}, bf16[768,768]{1,0:T(8,128)(2,1)}, u32[]{:S(2)}) copy-start(bf16[768,768]{1,0:T(8,128)(2,1)} %all-gather.11.cloned.1.call-done) | copy-start | bytes 3538948
  (31 other events, 78.9 us)
Sparse Core Ops, SparseCore 0:
  11.1 56.6 all-gather.16
  70.8 53.1 all-gather.10
  127.0 53.0 all-gather.14
  182.7 42.0 all-gather.18
  227.4 42.9 all-gather.12
  273.3 54.0 all-gather.20
  330.3 62.5 all-gather.22
  395.9 62.4 all-gather.24
  460.6 41.9 all-gather.26
  504.7 43.1 all-gather.28
  553.8 97.0 reduce-scatter.12
  657.4 97.9 reduce-scatter.18
  761.3 98.0 reduce-scatter.20
  865.9 98.0 reduce-scatter.22
  970.3 134.2 reduce-scatter.14
  1111.9 134.5 reduce-scatter.16
where the time goes:
time: 1260 us; the launch traced here: 1250 us
  waiting for transfers between devices  1020 us (81%)
  blocking collectives  104 us (8%)
  matrix products  73.3 us (6%)
  local copies, waits for them, and re-layouts  28.6 us (2%)
  between operations  14.6 us (1%)
    unnamed x19, waiting for transfers between devices  317 us
    reduce_scatter x1, waiting for transfers between devices, local(): lax.psum_scatter(w2_grad, ('dp', 'ctx'), scatter_dimension=0, tiled=True)  142 us
    reduce_scatter x1, waiting for transfers between devices, local(): lax.psum_scatter(w1_grad, ('dp', 'ctx'), scatter_dimension=0, tiled=True)  141 us
    unnamed x2, blocking collectives  79.8 us
    all_gather x1, waiting for transfers between devices, local(): lax.all_gather(w_in, ('dp', 'ctx'), axis=0, tiled=True)  62.7 us
    all_gather x1, waiting for transfers between devices, local(): lax.all_gather(w_key, ('dp', 'ctx'), axis=0, tiled=True)  58.3 us
    all_gather x1, waiting for transfers between devices, local(): lax.all_gather(w_back, ('dp', 'ctx'), axis=0, tiled=True)  57.1 us
    all_gather x1, waiting for transfers between devices, local(): lax.all_gather(w_query, ('dp', 'ctx'), axis=0, tiled=True)  51.5 us
  transfers between devices with their start and end apart: 16, of which 16 were waited for; matrix products, arithmetic and copies ran while one was open for 8% of the time, Pallas kernels for 0%

commit v1 on v0

--- a/solution.py
+++ b/solution.py
@@ -3,12 +3,639 @@
 import jax
 import jax.numpy as jnp
 from jax import lax
+from jax.experimental import pallas as pl
+from jax.experimental.pallas import tpu as pltpu
 from jax.sharding import PartitionSpec as P
 
+MESH = pl.DeviceIdType.MESH
+f32 = jnp.float32
+bf16 = jnp.bfloat16
 DH = 64
-
-
 epsilon = 1e-12
+
+
+def dot(a, b, ca=1, cb=0):
+    return lax.dot_general(a, b, (((ca,), (cb,)), ((), ())), preferred_element_type=f32)
+
+
+def norm_parts(values):
+    average = jnp.mean(values, axis=-1, keepdims=True)
+    centered = values - average
+    spread = jnp.mean(centered * centered, axis=-1, keepdims=True)
+    inverse = lax.rsqrt(spread + epsilon)
+    return centered * inverse, inverse
+
+
+def norm_back(incoming, scaled, inverse, gain):
+    along = incoming * gain
+    return inverse * (
+        along
+        - jnp.mean(along, axis=-1, keepdims=True)
+        - scaled * jnp.mean(along * scaled, axis=-1, keepdims=True)
+    )
+
+
+def layer_kernel(
+    tok, cot, wq, wk, wv, wo, wi, wb, vec,
+    lo_out, ig_out, dq_out, dk_out, dv_out, do_out, di_out, db_out, sm_out,
+    xr, cr, xg, pa, sa, si, sb, so, wa_f, wi_f, wb_f, wo8, wo_f,
+    sm0, smr, sm1, smz, sm2, sms, vf,
+    qs, kv, ee, mt, tot, mx, po, ro, hid, xh1, iv1, hg, gp, act, ds2, dg, dp, tg, dmt, dqt,
+    dkv, kvr, dall, ds1,
+    ga, ga_b, ra, s_a, za, fa, la,
+    gi, gi_b, ri, s_i, zi, fi,
+    gb, gb_b, rb, s_b, zb, fb,
+    go, go_b, r_o, s_o, z_o, fo,
+    igs, igr, gs0, gsr, gs1, gsz, gs2, gss,
+    ssem, rsem,
+):
+    d = lax.axis_index("dp")
+    k = lax.axis_index("ctx")
+    y, c = d // 2, d % 2
+    z, x = k // 2, k % 2
+    q = 2 * y + x
+    r = 8 * d + k
+
+    def dev(xx, yy, cc, zz):
+        return (2 * yy + cc, 2 * zz + xx)
+
+    def mate_q(m):
+        a, b = m % 2, m // 2
+        return 2 * ((y + b) % 2) + (x + a) % 2
+
+    def mate(m):
+        a, b = m % 2, m // 2
+        return dev((x + a) % 2, (y + b) % 2, c, z)
+
+    def plane(dz):
+        return dev(x, y, c, (z + dz) % 4)
+
+    sibling = dev(x, y, 1 - c, z)
+    pd, pz = 2 * (z % 2) + z // 2, 2 * c + y
+    partner = (pd, 2 * pz + x)
+    alone = (pd == d) & (pz == z)
+    cross = dev(c, y, x, z)
+    stays = x == c
+
+    bar = pltpu.get_barrier_semaphore()
+    near = [mate(1), mate(2), mate(3), sibling, plane(1), plane(2), plane(3)]
+    for other in near:
+        pl.semaphore_signal(bar, inc=1, device_id=other, device_id_type=MESH)
+
+    @pl.when(jnp.logical_not(alone))
+    def _():
+        pl.semaphore_signal(bar, inc=1, device_id=partner, device_id_type=MESH)
+
+    @pl.when(jnp.logical_not(stays))
+    def _():
+        pl.semaphore_signal(bar, inc=1, device_id=cross, device_id_type=MESH)
+
+    pl.semaphore_wait(bar, len(near) + 2 - alone.astype(jnp.int32) - stays.astype(jnp.int32))
+
+    sends = []
+
+    def send(src, dst, to, own=None):
+        i = len(sends)
+        cp = pltpu.make_async_remote_copy(
+            src_ref=src, dst_ref=dst, send_sem=ssem.at[i], recv_sem=rsem.at[i],
+            device_id=to, device_id_type=MESH,
+        )
+        if own is None:
+            cp.start()
+        else:
+            @pl.when(jnp.logical_not(own))
+            def _():
+                cp.start()
+
+            @pl.when(own)
+            def _():
+                dst[...] = src[...]
+        sends.append((cp, own))
+        return cp
+
+    def arrived(cp, own=None):
+        if own is None:
+            cp.wait_recv()
+        else:
+            @pl.when(jnp.logical_not(own))
+            def _():
+                cp.wait_recv()
+
+    def gather(ref):
+        return [send(ref.at[q], ref.at[q], mate(m)) for m in (1, 2, 3)]
+
+    def scatter(src, first, dst):
+        return [send(src.at[first + mate_q(m)], dst.at[m - 1], mate(m)) for m in (1, 2, 3)]
+
+    def all_in(copies):
+        for cp in copies:
+            cp.wait_recv()
+
+    c_tok = send(tok, xr, partner, alone)
+    for j in range(4):
+        cols = slice(192 * j, 192 * j + 192)
+        pa[j] = jnp.concatenate([wq[:, cols], wk[:, cols], wv[:, cols]], axis=1)
+    sa[q] = pa[q]
+    c_sa = [send(pa.at[mate_q(m)], sa.at[q], mate(m)) for m in (1, 2, 3)]
+    vec32 = vec[...].astype(f32)
+    row = lax.broadcasted_iota(jnp.int32, (16, 768), 0)
+    lane = lax.broadcasted_iota(jnp.int32, (16, 768), 1)
+    placed = jnp.where(row < 8, pltpu.roll(vec32, 24 * r, 1), 0.0)
+    b_in_row = pltpu.roll(vec32, 96 * (r % 8), 1)[8:9]
+    placed = placed + jnp.where(row == 8 + r // 8, b_in_row, 0.0)
+    sm0[...] = placed.astype(bf16)
+    c_sm = [send(sm0, smr.at[m - 1], mate(m)) for m in (1, 2, 3)]
+
+    def in_cols(j):
+        return wi.at[:, pl.ds(pl.multiple_of(768 * j, 768), 768)]
+
+    si[q] = wi[:, pl.ds(pl.multiple_of(768 * q, 768), 768)]
+    c_si = [send(in_cols(mate_q(m)), si.at[q], mate(m)) for m in (1, 2, 3)]
+    c_so = send(wo, so, cross, stays)
+    c_sb = send(wb, sb, cross, stays)
+
+    def own_rows(b, zz=None):
+        zz = z if zz is None else zz
+        return pl.ds(pl.multiple_of(384 * b + 192 * c + 48 * zz, 16), 48)
+
+    def core_rows(b, cc):
+        return pl.ds(pl.multiple_of(384 * b + 192 * cc, 16), 192)
+
+    def bundle(landed, full):
+        for b in range(2):
+            full[own_rows(b), :] = jnp.concatenate([landed[2 * b], landed[2 * b + 1]], axis=0)
+        return [
+            send(full.at[own_rows(b), :], full.at[own_rows(b), :], plane(dz))
+            for dz in (1, 2, 3)
+            for b in range(2)
+        ]
+
+    all_in(c_sa)
+    c_za = bundle(sa, wa_f)
+
+    all_in(c_sm)
+    total = sm0[...].astype(f32) + smr[0].astype(f32) + smr[1].astype(f32) + smr[2].astype(f32)
+    sm1[...] = total.astype(bf16)
+    c_smz = [send(sm1, smz.at[dz - 1], plane(dz)) for dz in (1, 2, 3)]
+
+    arrived(c_tok, alone)
+    xg[q] = xr[...]
+    c_xg = gather(xg)
+
+    all_in(c_smz)
+    total = sm1[...].astype(f32) + smz[0].astype(f32) + smz[1].astype(f32) + smz[2].astype(f32)
+    sm2[...] = total.astype(bf16)
+    c_sms = send(sm2, sms, sibling)
+
+    all_in(c_za)
+    c_ca = [
+        send(wa_f.at[core_rows(b, c), :], wa_f.at[core_rows(b, c), :], sibling) for b in range(2)
+    ]
+
+    arrived(c_so, stays)
+    slot_o = 2 * z + c
+    wo8[slot_o] = so[...]
+    c_zo = [send(wo8.at[slot_o], wo8.at[slot_o], plane(dz)) for dz in (1, 2, 3)]
+    all_in(c_si)
+    c_zi = bundle(si, wi_f)
+    arrived(c_sb, stays)
+
+    def b_rows(zz, cc):
+        return pl.ds(pl.multiple_of(96 * (2 * zz + cc), 96), 96)
+
+    wb_f[b_rows(z, c), :] = sb[...]
+    c_zb = [send(wb_f.at[b_rows(z, c), :], wb_f.at[b_rows(z, c), :], plane(dz)) for dz in (1, 2, 3)]
+    c_cot = send(cot, cr, partner, alone)
+
+    arrived(c_sms)
+    vf[...] = sm2[...].astype(f32) + sms[...].astype(f32)
+    b_out, gain1, shift1 = vf[2:3], vf[3:4], vf[4:5]
+    b_back, gain2, shift2 = vf[5:6], vf[6:7], vf[7:8]
+    turned = pltpu.roll(vf[...], lax.rem(768 - 192 * q, 768), 1)
+    b_qkv = jnp.concatenate(
+        [turned[0:1, :192], jnp.zeros((1, 192), f32), turned[1:2, :192]], axis=1
+    )
+    row1 = lax.broadcasted_iota(jnp.int32, (16, 768), 0)
+    b_in = jnp.sum(jnp.where(row1 == 8 + q, vf[...], 0.0), axis=0, keepdims=True)
+
+    all_in(c_ca)
+    c_kv = []
+    for m in range(4):
+        j = mate_q(m)
+        if m:
+            c_xg[m - 1].wait_recv()
+        out = dot(xg[j], wa_f[...]) + b_qkv
+        rows = pl.ds(pl.multiple_of(128 * j, 128), 128)
+        qs[rows, :] = (out[:, :192].astype(bf16).astype(f32) * 0.125).astype(bf16)
+        kv[c, rows, :] = out[:, 192:].astype(bf16)
+        c_kv.append(send(kv.at[c, rows, :], kv.at[c, rows, :], sibling))
+
+    mt[...] = jnp.zeros_like(mt)
+    tot[...] = jnp.zeros_like(tot)
+
+    def expo_rows(h, half, part):
+        return slice(1024 * h + 512 * half + 256 * part, 1024 * h + 512 * half + 256 * part + 256)
+
+    def forward_chunk(half, slot, part):
+        rows = slice(256 * part, 256 * part + 256)
+        keys_values = kv[half, rows, :]
+        for h in range(3):
+            key = keys_values[:, 64 * h:64 * h + 64]
+            value = keys_values[:, 192 + 64 * h:256 + 64 * h]
+            query = qs[:, 64 * h:64 * h + 64]
+            expo = jnp.exp(dot(key, query, 1, 1))
+            low = expo.astype(bf16)
+            ee[expo_rows(h, slot, part), :] = low
+            tot[h:h + 1, :] += jnp.sum(expo, axis=0, keepdims=True)
+            mt[64 * h:64 * h + 64, :] += dot(value, low, 0, 0)
+
+    forward_chunk(c, 0, 0)
+    forward_chunk(c, 0, 1)
+    all_in(c_kv)
+    forward_chunk(1 - c, 1, 0)
+    forward_chunk(1 - c, 1, 1)
+    for h in range(3):
+        part = slice(64 * h, 64 * h + 64)
+        mt[part, :] = mt[part, :] / tot[h:h + 1, :]
+    mx[...] = jnp.transpose(mt[...]).astype(bf16)
+
+    all_in(c_zo)
+    c_co = [send(wo8.at[2 * zz + c], wo8.at[2 * zz + c], sibling) for zz in range(4)]
+    all_in(c_co)
+    for j in range(8):
+        wo_f[24 * j:24 * j + 24, :] = wo8[j]
+
+    def project(m, _):
+        j = mate_q(m)
+        rows = pl.ds(pl.multiple_of(128 * j, 128), 128)
+        po[j] = dot(mx[rows, :], wo_f[...]).astype(bf16)
+        return 0
+
+    lax.fori_loop(1, 4, project, 0)
+    c_ro = scatter(po, 0, ro.at[0])
+    own = pl.ds(pl.multiple_of(128 * q, 128), 128)
+    attn = dot(mx[own, :], wo_f[...]) + b_out
+    all_in(c_ro)
+    attn = attn + ro[0, 0].astype(f32) + ro[0, 1].astype(f32) + ro[0, 2].astype(f32)
+    x32 = xr[...].astype(f32)
+    stream = x32 + attn
+    squares_x = jnp.sum(x32 * x32)
+    squares_s = jnp.sum(stream * stream)
+    scaled, inverse = norm_parts(stream)
+    xh1[...] = scaled
+    iv1[...] = jnp.broadcast_to(inverse, iv1.shape)
+    hidden = scaled * gain1 + shift1
+    hid[...] = hidden
+    hg[q] = hidden.astype(bf16)
+    c_hg = gather(hg)
+
+    all_in(c_zi)
+    c_ci = [
+        send(wi_f.at[core_rows(b, c), :], wi_f.at[core_rows(b, c), :], sibling) for b in range(2)
+    ]
+    all_in(c_zb)
+    c_cb = [send(wb_f.at[b_rows(zz, c), :], wb_f.at[b_rows(zz, c), :], sibling) for zz in range(4)]
+    all_in(c_ci)
+    all_in(c_cb)
+
+    def ffn(j):
+        pre = dot(hg[j], wi_f[...]) + b_in
+        phi = 0.5 + 0.5 * lax.erf(pre * 0.7071067811865476)
+        gp[j] = phi + pre * jnp.exp(-0.5 * pre * pre) * 0.3989422804014327
+        act[j] = (pre * phi).astype(bf16)
+        return dot(act[j], wb_f[...])
+
+    own_part = ffn(q)
+    c_ffn = []
+    for m in (1, 2, 3):
+        c_hg[m - 1].wait_recv()
+        j = mate_q(m)
+        po[4 + j] = ffn(j).astype(bf16)
+        c_ffn.append(send(po.at[4 + j], ro.at[1, m - 1], mate(m)))
+    all_in(c_ffn)
+    out = own_part + b_back + ro[1, 0].astype(f32) + ro[1, 1].astype(f32) + ro[1, 2].astype(f32)
+    scaled2, inverse2 = norm_parts(hid[...] + out)
+    igs[0] = (scaled2 * gain2 + shift2).astype(bf16)
+    arrived(c_cot, alone)
+    dy = cr[...].astype(f32)
+    gain2_grad = jnp.sum(dy * scaled2, axis=0, keepdims=True)
+    shift2_grad = jnp.sum(dy, axis=0, keepdims=True)
+    dsum2 = norm_back(dy, scaled2, inverse2, gain2)
+    ds2[...] = dsum2
+    low = dsum2.astype(bf16)
+    dg[q] = low
+    back_grad = jnp.sum(low.astype(f32), axis=0, keepdims=True)
+    c_dg = gather(dg)
+    c_lo = send(igs.at[0], lo_out, partner, alone)
+
+    def ffn_back(j):
+        dact = dot(dg[j], wb_f[...], 1, 1)
+        dp[j] = (dact * gp[j]).astype(bf16)
+        return dot(dp[j], wi_f[...], 1, 1)
+
+    own_part = ffn_back(q)
+    c_dh = []
+    for m in (1, 2, 3):
+        c_dg[m - 1].wait_recv()
+        j = mate_q(m)
+        po[8 + j] = ffn_back(j).astype(bf16)
+        c_dh.append(send(po.at[8 + j], ro.at[2, m - 1], mate(m)))
+
+    def weight_grad(left, right, out, low, rows):
+        for i in range(rows // 256):
+            cols = slice(256 * i, 256 * i + 256)
+            part = dot(left[:, cols], right, 0, 0)
+            out[cols, :] = part
+            low[cols, :] = part.astype(bf16)
+
+    def flat(ref):
+        return ref[...].reshape(512, ref.shape[-1])
+
+    weight_grad(flat(act), flat(dg), gb, gb_b, 768)
+    c_rb = [send(gb_b.at[b_rows(zz, 1 - c), :], rb.at[zz], sibling) for zz in range(4)]
+    weight_grad(flat(hg), flat(dp), gi, gi_b, 768)
+    c_ri = [send(gi_b.at[core_rows(b, 1 - c), :], ri.at[b], sibling) for b in range(2)]
+    in_grad = jnp.sum(flat(dp).astype(f32), axis=0, keepdims=True)
+
+    all_in(c_dh)
+    dhidden = (
+        ds2[...] + own_part + ro[2, 0].astype(f32) + ro[2, 1].astype(f32) + ro[2, 2].astype(f32)
+    )
+    gain1_grad = jnp.sum(dhidden * xh1[...], axis=0, keepdims=True)
+    shift1_grad = jnp.sum(dhidden, axis=0, keepdims=True)
+    dsum1 = norm_back(dhidden, xh1[...], iv1[:, :1], gain1)
+    ds1[...] = dsum1
+    low = dsum1.astype(bf16)
+    tg[q] = low
+    out_grad = jnp.sum(low.astype(f32), axis=0, keepdims=True)
+    c_tg = gather(tg)
+
+    def row_sums(c_in, partial_sum, recv, low, landing):
+        all_in(c_in)
+        copies = []
+        for zz in range(4):
+            rows = b_rows(zz, c)
+            low[zz] = (partial_sum[rows, :] + recv[zz].astype(f32)).astype(bf16)
+        for dz in (1, 2, 3):
+            copies.append(send(low.at[(z + dz) % 4], landing.at[dz - 1], plane(dz)))
+        return copies
+
+    def col_sums(c_in, partial_sum, recv, low, landing):
+        all_in(c_in)
+        for zz in range(4):
+            for b in range(2):
+                mine = partial_sum[own_rows(b, zz), :]
+                theirs = recv[b, 48 * zz:48 * zz + 48, :].astype(f32)
+                low[zz, b] = (mine + theirs).astype(bf16)
+        return [send(low.at[(z + dz) % 4], landing.at[dz - 1], plane(dz)) for dz in (1, 2, 3)]
+
+    c_zgb = row_sums(c_rb, gb, rb, s_b, zb)
+    c_zgi = col_sums(c_ri, gi, ri, s_i, zi)
+
+    def mixed_back(j):
+        cols = pl.ds(pl.multiple_of(128 * j, 128), 128)
+        dmt[:, cols] = dot(wo_f[...], tg[j], 1, 1)
+
+    mixed_back(q)
+    for m in (1, 2, 3):
+        c_tg[m - 1].wait_recv()
+        mixed_back(mate_q(m))
+    part = dot(mt[...].astype(bf16), flat(tg))
+    for j in range(8):
+        go[j] = part[24 * j:24 * j + 24]
+        go_b[j] = part[24 * j:24 * j + 24].astype(bf16)
+    c_rgo = [send(go_b.at[2 * zz + 1 - c], r_o.at[zz], sibling) for zz in range(4)]
+
+    dqt[...] = jnp.zeros_like(dqt)
+
+    def backward_chunk(half, slot, part):
+        rows = slice(256 * part, 256 * part + 256)
+        keys_values = kv[half, rows, :]
+        dkeys, dvalues = [], []
+        for h in range(3):
+            span = slice(64 * h, 64 * h + 64)
+            key = keys_values[:, span]
+            value = keys_values[:, 192 + 64 * h:256 + 64 * h]
+            query = qs[:, span]
+            over = 1.0 / tot[h:h + 1, :]
+            dmixed = dmt[span, :]
+            dsummed = (dmixed * over).astype(bf16)
+            delta = jnp.sum(dmixed * mt[span, :], axis=0, keepdims=True) * over
+            expo = ee[expo_rows(h, slot, part), :]
+            across = dot(value, dsummed)
+            slopes = (expo.astype(f32) * (across - delta)).astype(bf16)
+            dvalues.append(dot(expo, dsummed, 1, 1))
+            dkeys.append(dot(slopes, query))
+            dqt[span, :] += dot(key, slopes, 0, 0)
+        dkv[half, rows, :] = jnp.concatenate(dkeys + dvalues, axis=1)
+
+    backward_chunk(1 - c, 1, 0)
+    backward_chunk(1 - c, 1, 1)
+    c_dkv = send(dkv.at[1 - c], kvr, sibling)
+    backward_chunk(c, 0, 0)
+    backward_chunk(c, 0, 1)
+    dall[:, :192] = jnp.transpose(dqt[...] * 0.125).astype(bf16)
+    arrived(c_dkv)
+    dall[:, 192:] = (dkv[c] + kvr[...]).astype(bf16)
+
+    def input_back(m, _):
+        j = mate_q(m)
+        rows = pl.ds(pl.multiple_of(128 * j, 128), 128)
+        po[12 + j] = dot(dall[rows, :], wa_f[...], 1, 1).astype(bf16)
+        return 0
+
+    lax.fori_loop(1, 4, input_back, 0)
+    c_dx = scatter(po, 12, ro.at[3])
+    own_part = dot(dall[own, :], wa_f[...], 1, 1)
+
+    weight_grad(flat(xg), dall[...], ga, ga_b, 768)
+    c_rga = [send(ga_b.at[core_rows(b, 1 - c), :], ra.at[b], sibling) for b in range(2)]
+    sums = jnp.sum(dall[...].astype(f32), axis=0, keepdims=True)
+
+    rest = jnp.zeros((1, 576), f32)
+    head_rows = jnp.concatenate(
+        [jnp.concatenate([sums[:, :192], rest], axis=1),
+         jnp.concatenate([sums[:, 384:], rest], axis=1),
+         jnp.zeros((6, 768), f32)], axis=0,
+    )
+    gs0[...] = jnp.zeros_like(gs0)
+    gs0[0:8, :] = pltpu.roll(head_rows, 192 * q, 1)
+    gs0[2:3, :] = out_grad
+    gs0[3:4, :] = gain1_grad
+    gs0[4:5, :] = shift1_grad
+    gs0[5:6, :] = back_grad
+    gs0[6:7, :] = gain2_grad
+    gs0[7:8, :] = shift2_grad
+    row2 = lax.broadcasted_iota(jnp.int32, (8, 768), 0)
+    gs0[8:16, :] = (
+        jnp.where(row2 == q, in_grad, 0.0)
+        + jnp.where(row2 == 4, squares_x, 0.0)
+        + jnp.where(row2 == 5, squares_s, 0.0)
+    )
+    c_gs = [send(gs0, gsr.at[m - 1], mate(m)) for m in (1, 2, 3)]
+
+    all_in(c_rgo)
+    for zz in range(4):
+        s_o[zz] = (go[2 * zz + c] + r_o[zz].astype(f32)).astype(bf16)
+    c_zgo = [send(s_o.at[(z + dz) % 4], z_o.at[dz - 1], plane(dz)) for dz in (1, 2, 3)]
+    c_zga = col_sums(c_rga, ga, ra, s_a, za)
+
+    all_in(c_dx)
+    input_grad = (
+        ds1[...] + own_part + ro[3, 0].astype(f32) + ro[3, 1].astype(f32) + ro[3, 2].astype(f32)
+    )
+    igs[1] = input_grad.astype(bf16)
+    c_ig = send(igs.at[1], igr, partner, alone)
+
+    all_in(c_gs)
+    gs1[...] = gs0[...] + gsr[0] + gsr[1] + gsr[2]
+    c_gsz = [send(gs1, gsz.at[dz - 1], plane(dz)) for dz in (1, 2, 3)]
+
+    all_in(c_zgb)
+    fb[...] = (
+        s_b[z].astype(f32) + zb[0].astype(f32) + zb[1].astype(f32) + zb[2].astype(f32)
+    )
+    c_fb = send(fb, db_out, cross, stays)
+
+    def col_final(c_in, low, landing, out):
+        all_in(c_in)
+        for b in range(2):
+            whole = (
+                low[z, b].astype(f32) + landing[0, b].astype(f32)
+                + landing[1, b].astype(f32) + landing[2, b].astype(f32)
+            )
+            out[2 * b] = whole[:24]
+            out[2 * b + 1] = whole[24:]
+
+    col_final(c_zgi, s_i, zi, fi)
+
+    def out_cols(j):
+        return di_out.at[:, pl.ds(pl.multiple_of(768 * j, 768), 768)]
+
+    c_fi = [send(fi.at[mate_q(m)], out_cols(q), mate(m)) for m in (1, 2, 3)]
+    di_out[:, pl.ds(pl.multiple_of(768 * q, 768), 768)] = fi[q]
+
+    all_in(c_zgo)
+    fo[...] = (
+        s_o[z].astype(f32) + z_o[0].astype(f32) + z_o[1].astype(f32) + z_o[2].astype(f32)
+    )
+    c_fo = send(fo, do_out, cross, stays)
+
+    all_in(c_gsz)
+    gs2[...] = gs1[...] + gsz[0] + gsz[1] + gsz[2]
+    c_gss = send(gs2, gss, sibling)
+
+    col_final(c_zga, s_a, za, fa)
+    la[q] = fa[q]
+    c_fa = [send(fa.at[mate_q(m)], la.at[q], mate(m)) for m in (1, 2, 3)]
+
+    arrived(c_ig, alone)
+    ig_out[...] = igr[...].astype(f32)
+
+    arrived(c_gss)
+    whole = gs2[...] + gss[...]
+    sm_out[0:8, :] = pltpu.roll(whole, lax.rem(768 - 24 * r, 768), 1)[:8, :128]
+    mine = jnp.sum(
+        jnp.where(lax.broadcasted_iota(jnp.int32, (16, 768), 0) == 8 + r // 8, whole, 0.0),
+        axis=0, keepdims=True,
+    )
+    mine = pltpu.roll(jnp.broadcast_to(mine, (8, 768)), lax.rem(768 - 96 * (r % 8), 768), 1)
+    row3 = lax.broadcasted_iota(jnp.int32, (8, 128), 0)
+    sm_out[8:16, :] = jnp.where(row3 < 4, mine[:, :128], whole[8:16, :128])
+
+    all_in(c_fa)
+    for j in range(4):
+        cols = slice(192 * j, 192 * j + 192)
+        dq_out[:, cols] = la[j, :, :192]
+        dk_out[:, cols] = la[j, :, 192:384]
+        dv_out[:, cols] = la[j, :, 384:]
+
+    arrived(c_lo, alone)
+    arrived(c_fb, stays)
+    arrived(c_fo, stays)
+    all_in(c_fi)
+    for cp, own_copy in sends:
+        if own_copy is None:
+            cp.wait_send()
+        else:
+            @pl.when(jnp.logical_not(own_copy))
+            def _():
+                cp.wait_send()
+
+
+COPIES = 200
+
+
+def fused(
+    tokens, w_query, w_key, w_value, w_out, b_query, b_value, b_out, norm1_gain, norm1_shift,
+    w_in, b_in, w_back, b_back, norm2_gain, norm2_shift, cotangent,
+):
+    vectors = jnp.stack(
+        [b_query, b_value, b_out, norm1_gain, norm1_shift, b_back, norm2_gain, norm2_shift]
+    )
+    vec = jnp.concatenate(
+        [
+            jnp.pad(vectors, ((0, 0), (0, 768 - 24))),
+            jnp.pad(b_in[None, :], ((0, 7), (0, 768 - 96))),
+        ],
+        axis=0,
+    )
+    vm = pl.BlockSpec(memory_space=pltpu.VMEM)
+
+    def v(*shape, t=bf16):
+        return pltpu.VMEM(shape, t)
+
+    outs = (
+        jax.ShapeDtypeStruct((128, 768), bf16),
+        jax.ShapeDtypeStruct((128, 768), f32),
+        jax.ShapeDtypeStruct((24, 768), f32),
+        jax.ShapeDtypeStruct((24, 768), f32),
+        jax.ShapeDtypeStruct((24, 768), f32),
+        jax.ShapeDtypeStruct((24, 768), f32),
+        jax.ShapeDtypeStruct((24, 3072), f32),
+        jax.ShapeDtypeStruct((96, 768), f32),
+        jax.ShapeDtypeStruct((16, 128), f32),
+    )
+    scratch = [
+        v(128, 768), v(128, 768), v(4, 128, 768), v(4, 24, 576), v(4, 24, 576), v(4, 24, 768),
+        v(96, 768), v(24, 768), v(768, 576), v(768, 768), v(768, 768), v(8, 24, 768), v(192, 768),
+        v(16, 768), v(3, 16, 768), v(16, 768), v(3, 16, 768), v(16, 768), v(16, 768),
+        v(16, 768, t=f32),
+        v(512, 192), v(2, 512, 384), v(3072, 512), v(192, 512, t=f32), v(8, 512, t=f32),
+        v(512, 192), v(16, 128, 768), v(4, 3, 128, 768),
+        v(128, 768, t=f32), v(128, 768, t=f32), v(128, 128, t=f32), v(4, 128, 768),
+        v(4, 128, 768, t=f32), v(4, 128, 768), v(128, 768, t=f32), v(4, 128, 768),
+        v(4, 128, 768), v(4, 128, 768), v(192, 512, t=f32), v(192, 512, t=f32),
+        v(2, 512, 384, t=f32), v(512, 384, t=f32), v(512, 576), v(128, 768, t=f32),
+        v(768, 576, t=f32), v(768, 576), v(2, 192, 576), v(4, 2, 48, 576), v(3, 2, 48, 576),
+        v(4, 24, 576, t=f32), v(4, 24, 576, t=f32),
+        v(768, 768, t=f32), v(768, 768), v(2, 192, 768), v(4, 2, 48, 768), v(3, 2, 48, 768),
+        v(4, 24, 768, t=f32),
+        v(768, 768, t=f32), v(768, 768), v(4, 96, 768), v(4, 96, 768), v(3, 96, 768),
+        v(96, 768, t=f32),
+        v(8, 24, 768, t=f32), v(8, 24, 768), v(4, 24, 768), v(4, 24, 768), v(3, 24, 768),
+        v(24, 768, t=f32),
+        v(2, 128, 768), v(128, 768), v(16, 768, t=f32), v(3, 16, 768, t=f32),
+        v(16, 768, t=f32), v(3, 16, 768, t=f32), v(16, 768, t=f32), v(16, 768, t=f32),
+        pltpu.SemaphoreType.DMA((COPIES,)), pltpu.SemaphoreType.DMA((COPIES,)),
+    ]
+    lo, ig, dq, dk, dv, do, di, db, sm = pl.pallas_call(
+        layer_kernel,
+        out_shape=outs,
+        in_specs=[vm] * 9,
+        out_specs=[vm] * 9,
+        scratch_shapes=scratch,
+        compiler_params=pltpu.CompilerParams(
+            collective_id=0, has_side_effects=True, vmem_limit_bytes=60 << 20
+        ),
+        name="layer",
+    )(tokens, cotangent, w_query, w_key, w_value, w_out, w_in, w_back, vec)
+    small = [sm[i, :24] for i in range(8)]
+    rms = jnp.sqrt(jnp.stack([sm[12, 0], sm[13, 0]]) / (4096 * 768))
+    return (
+        lo, ig, dq, dk, dv, do, small[0], small[1], small[2], small[3], small[4], di, sm[8, :96],
+        db, small[5], small[6], small[7], rms,
+    )
 
 
 def normalize(values, gain, shift):
@@ -34,7 +661,7 @@
     return row_array.reshape(row_array.shape[0], -1, DH)
 
 
-def local(
+def general(
     tokens,
     w_query,
     w_key,
@@ -235,43 +862,8 @@
 
 
 def solution(mesh):
-    in_specs = (
-        P(("dp", "ctx"), None),
-        P(("dp", "ctx"), None),
-        P(("dp", "ctx"), None),
-        P(("dp", "ctx"), None),
-        P(("dp", "ctx"), None),
-        P(("dp", "ctx")),
-        P(("dp", "ctx")),
-        P(("dp", "ctx")),
-        P(("dp", "ctx")),
-        P(("dp", "ctx")),
-        P(("dp", "ctx"), None),
-        P(("dp", "ctx")),
-        P(("dp", "ctx"), None),
-        P(("dp", "ctx")),
-        P(("dp", "ctx")),
-        P(("dp", "ctx")),
-        P(("dp", "ctx"), None),
-    )
-    out_specs = (
-        P(("dp", "ctx"), None),
-        P(("dp", "ctx"), None),
-        P(("dp", "ctx"), None),
-        P(("dp", "ctx"), None),
-        P(("dp", "ctx"), None),
-        P(("dp", "ctx"), None),
-        P(("dp", "ctx")),
-        P(("dp", "ctx")),
-        P(("dp", "ctx")),
-        P(("dp", "ctx")),
-        P(("dp", "ctx")),
-        P(("dp", "ctx"), None),
-        P(("dp", "ctx")),
-        P(("dp", "ctx"), None),
-        P(("dp", "ctx")),
-        P(("dp", "ctx")),
-        P(("dp", "ctx")),
-        P(),
-    )
-    return jax.shard_map(local, mesh=mesh, in_specs=in_specs, out_specs=out_specs, check_vma=False)
+    rows, flat = P(("dp", "ctx"), None), P(("dp", "ctx"))
+    in_specs = (rows,) * 5 + (flat,) * 5 + (rows, flat, rows) + (flat,) * 3 + (rows,)
+    out_specs = (rows,) * 6 + (flat,) * 5 + (rows, flat, rows) + (flat,) * 3 + (P(),)
+    body = fused if (mesh.shape["dp"], mesh.shape["ctx"]) == (4, 8) else general
+    return jax.shard_map(body, mesh=mesh, in_specs=in_specs, out_specs=out_specs, check_vma=False)

time: 1260 us -> 167 us (0.13)
  the two profiles are of different devices: /device:TPU:1 before, /device:TPU:0 now
where the time goes in v1:
time: 167 us; the launch traced here: 166 us
  Pallas kernels  151 us (90%)
  local copies, waits for them, and re-layouts  12.5 us (7%)
  other arithmetic  2.5 us (1%)
    pallas_call x1, Pallas kernels, fused(): pl.pallas_call(layer_kernel, out_shape=outs, in_specs=[vm] * 9, out_specs...  151 us
    unnamed x40, local copies, waits for them, and re-layouts  8.44 us

profile of v1, /device:TPU:0, one launch (start us, length us, event | category | flops | bytes accessed | tf_op | source)
XLA Modules:
  0.0 166.4 jit_solution(3781217005947838698)
XLA Ops:
  0.7 0.0 copy-start.14
  0.7 0.0 copy-start.10
  0.7 0.0 copy-start.11
  0.7 0.0 copy-start.12
  0.7 0.0 copy-start.13
  0.7 0.6 copy-done.14
  1.3 0.0 copy-done.10
  1.3 0.0 copy-done.11
  1.3 0.0 copy-done.12
  1.4 0.0 copy-done.13
  1.4 0.0 copy-done.7
  1.4 0.0 copy-done.8
  1.4 0.0 copy-done.9
  1.5 0.6 copy-done.15
  2.1 0.6 fusion.2.vec
  2.7 150.7 %layer.1 = (bf16[128,768]{1,0:T(8,128)(2,1)}, f32[128,768]{1,0:T(8,128)}, f32[24,768]{1,0:T(8,128)}, f32[24,768]{1,0:T(8,128)}, f32[24,768]{1,0:T(8,128)}, /*ind...) custom-call(bf16[128,768]{1,0:T(8,128)(2,1)} %tok.1, bf16[128,768]{1,0:T(8,128)(2,1)} %cot.1, ...), custom_call_target="tpu_custom_call" | custom-call | tf_op jit(solution)/shard_map/layer/pallas_call | solution.py:622
  153.4 1.2 slice_bitcast_fusion.3
  154.6 1.3 fusion.4
  155.9 1.5 slice_bitcast_fusion
  157.4 1.9 %fusion.3 = f32[2]{0:T(128)} fusion(f32[1]{0:T(128)} %bitcast.19, f32[1]{0:T(128)} %bitcast.18), kind=kLoop, calls=%fused_computation.6 | loop fusion | flops 4 | bytes 16 | tf_op jit(solution)/shard_map/sqrt | solution.py:634
  159.3 1.6 copy.43
  160.9 0.7 copy.44
  161.7 0.1 copy-done.6
  161.8 0.6 copy.45
  162.4 0.0 copy-done.5
  162.4 0.6 copy.46
  163.1 0.6 copy.47
  163.7 0.3 copy-done.3
  164.0 0.6 copy.48
  164.6 0.7 copy.49
  165.3 0.4 copy-done.1
  165.7 0.7 copy.50
  (15 shorter events, 0.1 us)
Async XLA Ops:
  0.7 0.7 copy-start.14
  0.7 0.7 copy-start.10
  0.7 0.7 copy-start.11
  0.7 0.7 copy-start.12
  0.7 0.7 copy-start.13
  0.7 0.7 copy-start.7
  0.7 0.7 copy-start.8
  0.7 0.7 copy-start.9
  1.4 0.7 copy-start.15
  153.4 7.5 %copy-start = (f32[128,768]{1,0:T(8,128)S(1)}, f32[128,768]{1,0:T(8,128)}, u32[]{:S(2)}) copy-start(f32[128,768]{1,0:T(8,128)} %get-tuple-element.65) | copy-start | bytes 1179652
  160.9 0.9 copy-start.6
  160.9 1.5 copy-start.5
  160.9 2.2 %copy-start.4 = (f32[24,768]{1,0:T(8,128)S(1)}, f32[24,768]{1,0:T(8,128)}, u32[]{:S(2)}) copy-start(f32[24,768]{1,0:T(8,128)} %get-tuple-element.68) | copy-start | bytes 221188
  161.8 2.8 %copy-start.2 = (f32[24,3072]{1,0:T(8,128)S(1)}, f32[24,3072]{1,0:T(8,128)}, u32[]{:S(2)}) copy-start(f32[24,3072]{1,0:T(8,128)} %get-tuple-element.75) | copy-start | bytes 884740
  163.1 0.9 copy-start.3
  164.6 1.1 copy-start.1

commit v2 on v1

--- a/solution.py
+++ b/solution.py
@@ -12,6 +12,7 @@
 bf16 = jnp.bfloat16
 DH = 64
 epsilon = 1e-12
+COPIES = 87
 
 
 def dot(a, b, ca=1, cb=0):
@@ -35,18 +36,60 @@
     )
 
 
+def wide(*refs):
+    total = refs[0].astype(f32)
+    for ref in refs[1:]:
+        total = total + ref.astype(f32)
+    return total
+
+
+class Copy:
+    def __init__(self, parts, whole, goes, comes):
+        self.parts, self.whole, self.goes, self.comes, self.waited = parts, whole, goes, comes, False
+
+    def _if(self, condition, act):
+        if condition is None:
+            act()
+        else:
+            pl.when(condition)(act)
+
+    def start(self):
+        def act():
+            for part in self.parts:
+                part.start()
+
+        self._if(self.goes, act)
+
+    def landed(self):
+        self.waited = True
+        self._if(self.comes, self.whole.wait_recv)
+
+    def left(self):
+        self._if(self.goes, self.whole.wait_send)
+
+
+def landed(copies):
+    for copy in copies:
+        copy.landed()
+
+
+ORDER = [
+    16 * ((b // 8) % 2) + 4 * (2 * (b // 16) + b % 2) + (b % 8) // 2 for b in range(32)
+]
+
+
 def layer_kernel(
-    tok, cot, wq, wk, wv, wo, wi, wb, vec,
-    lo_out, ig_out, dq_out, dk_out, dv_out, do_out, di_out, db_out, sm_out,
-    xr, cr, xg, pa, sa, si, sb, so, wa_f, wi_f, wb_f, wo8, wo_f,
-    sm0, smr, sm1, smz, sm2, sms, vf,
-    qs, kv, ee, mt, tot, mx, po, ro, hid, xh1, iv1, hg, gp, act, ds2, dg, dp, tg, dmt, dqt,
-    dkv, kvr, dall, ds1,
-    ga, ga_b, ra, s_a, za, fa, la,
+    tok, cot, wq, wk, wv, wo, wi, wb, bq, bv, bo, g1, s1, bb, g2, s2, bi,
+    lo_out, igr, la, do_out, di_out, db_out, sm_out,
+    xr, cr, xg, pa, sa, si, sb, wa_f, wi_f, wb_f, wo_b, wo_f,
+    vec32, sm0, smr, sm1, smz, sm2, sms, vf,
+    qs, kv, ee, mt, tot, mxs, mix, po, ro, hid, xh1, iv1, hg, gp, act, ds2, dg, dp, da, dms, dmi,
+    dmt, dqt, dkv, kvr, dall, ds1,
+    ga, ga_b, ra, s_a, za, fa,
     gi, gi_b, ri, s_i, zi, fi,
     gb, gb_b, rb, s_b, zb, fb,
-    go, go_b, r_o, s_o, z_o, fo,
-    igs, igr, gs0, gsr, gs1, gsz, gs2, gss,
+    go_b, r_o, s_o, p_o, t_o, z_o,
+    los, igs, gs0, gsr, gs1, gsz, gs2, gss,
     ssem, rsem,
 ):
     d = lax.axis_index("dp")
@@ -74,19 +117,21 @@
     pd, pz = 2 * (z % 2) + z // 2, 2 * c + y
     partner = (pd, 2 * pz + x)
     alone = (pd == d) & (pz == z)
+    moves = jnp.logical_not(alone)
     cross = dev(c, y, x, z)
     stays = x == c
+    crosses = jnp.logical_not(stays)
 
     bar = pltpu.get_barrier_semaphore()
     near = [mate(1), mate(2), mate(3), sibling, plane(1), plane(2), plane(3)]
     for other in near:
         pl.semaphore_signal(bar, inc=1, device_id=other, device_id_type=MESH)
 
-    @pl.when(jnp.logical_not(alone))
+    @pl.when(moves)
     def _():
         pl.semaphore_signal(bar, inc=1, device_id=partner, device_id_type=MESH)
 
-    @pl.when(jnp.logical_not(stays))
+    @pl.when(crosses)
     def _():
         pl.semaphore_signal(bar, inc=1, device_id=cross, device_id_type=MESH)
 
@@ -94,147 +139,216 @@
 
     sends = []
 
-    def send(src, dst, to, own=None):
+    def send(*transfers, size=None, goes=None, comes=None):
         i = len(sends)
-        cp = pltpu.make_async_remote_copy(
-            src_ref=src, dst_ref=dst, send_sem=ssem.at[i], recv_sem=rsem.at[i],
-            device_id=to, device_id_type=MESH,
+
+        def copy_of(src, dst, to):
+            return pltpu.make_async_remote_copy(
+                src_ref=src, dst_ref=dst, send_sem=ssem.at[i], recv_sem=rsem.at[i],
+                device_id=to, device_id_type=MESH,
+            )
+
+        parts = [copy_of(*transfer) for transfer in transfers]
+        whole = parts[0] if size is None else copy_of(size, size, transfers[0][2])
+        copy = Copy(parts, whole, goes, comes)
+        copy.start()
+        sends.append(copy)
+        return copy
+
+    def swap(src, dst, to, here):
+        there = jnp.logical_not(here)
+        copy = send((src, dst, to), goes=there, comes=there)
+
+        @pl.when(here)
+        def _():
+            dst[...] = src[...]
+
+        return copy
+
+    def gather(ref):
+        return [send((ref.at[q], ref.at[q], mate(m))) for m in (1, 2, 3)]
+
+    def to_mates(src, dst):
+        return send(
+            *[(src.at[mate_q(m)], dst.at[q], mate(m)) for m in (1, 2, 3)], size=src.at[pl.ds(0, 3)]
         )
-        if own is None:
-            cp.start()
-        else:
-            @pl.when(jnp.logical_not(own))
-            def _():
-                cp.start()
-
-            @pl.when(own)
-            def _():
-                dst[...] = src[...]
-        sends.append((cp, own))
-        return cp
-
-    def arrived(cp, own=None):
-        if own is None:
-            cp.wait_recv()
-        else:
-            @pl.when(jnp.logical_not(own))
-            def _():
-                cp.wait_recv()
-
-    def gather(ref):
-        return [send(ref.at[q], ref.at[q], mate(m)) for m in (1, 2, 3)]
-
-    def scatter(src, first, dst):
-        return [send(src.at[first + mate_q(m)], dst.at[m - 1], mate(m)) for m in (1, 2, 3)]
-
-    def all_in(copies):
-        for cp in copies:
-            cp.wait_recv()
-
-    c_tok = send(tok, xr, partner, alone)
+
+    def share(src, dst, others):
+        return send(*[(src, dst.at[i], other) for i, other in enumerate(others)], size=dst)
+
+    mates = [mate(1), mate(2), mate(3)]
+    planes = [plane(1), plane(2), plane(3)]
+    ends = (z == 0) | (z == 3)
+    middle = jnp.logical_not(ends)
+
+    def spread(part, size):
+        def copy(to, goes, comes):
+            return send(*[(ref, ref, to) for ref in part(z)], size=size, goes=goes, comes=comes)
+
+        return [
+            copy(plane(2), None, None), copy(plane(1), z < 3, z > 0), copy(plane(3), z > 0, z < 3)
+        ]
+
+    def spread_on(copies, part, size):
+        copies[0].landed()
+        to = dev(x, y, c, lax.rem(3 * (z + 3), 4))
+        far = lax.rem(z + 2, 4)
+        last = send(*[(ref, ref, to) for ref in part(far)], size=size, goes=middle, comes=ends)
+        return copies[1:] + [last]
+
+    def collect(low, landing):
+        return [
+            send((low.at[3 - z], landing.at[3], dev(x, y, c, lax.rem(z + 1 + 2 * (z // 3), 4))),
+                 goes=ends, comes=middle),
+            send((low.at[lax.rem(z + 1, 4)], landing.at[0], plane(1)), goes=z < 3, comes=z > 0),
+            send((low.at[lax.rem(z + 3, 4)], landing.at[1], plane(3)), goes=z > 0, comes=z < 3),
+        ]
+
+    def collect_on(copies, low, landing):
+        copies[0].landed()
+        far = lax.rem(z + 2, 4)
+
+        @pl.when(middle)
+        def _():
+            low[far] = wide(low[far], landing[3]).astype(bf16)
+
+        return copies[1:] + [send((low.at[far], landing.at[2], plane(2)))]
+
+    @pl.when(z == 0)
+    def _():
+        for ref in (za, zi, zb, z_o):
+            ref[0] = jnp.zeros_like(ref[0])
+
+    @pl.when(z == 3)
+    def _():
+        for ref in (za, zi, zb, z_o):
+            ref[1] = jnp.zeros_like(ref[1])
+
+    halves = [slice(0, 64), slice(64, 128)]
+    c_tok = [swap(tok.at[rows, :], xr.at[rows, :], partner, alone) for rows in halves]
     for j in range(4):
         cols = slice(192 * j, 192 * j + 192)
         pa[j] = jnp.concatenate([wq[:, cols], wk[:, cols], wv[:, cols]], axis=1)
     sa[q] = pa[q]
-    c_sa = [send(pa.at[mate_q(m)], sa.at[q], mate(m)) for m in (1, 2, 3)]
-    vec32 = vec[...].astype(f32)
+    c_sa = to_mates(pa, sa)
+    vec32[...] = jnp.zeros_like(vec32)
+    for i, ref in enumerate((bq, bv, bo, g1, s1, bb, g2, s2)):
+        vec32[i:i + 1, :24] = ref[...].astype(f32)
+    vec32[8:9, :96] = bi[...].astype(f32)
     row = lax.broadcasted_iota(jnp.int32, (16, 768), 0)
-    lane = lax.broadcasted_iota(jnp.int32, (16, 768), 1)
-    placed = jnp.where(row < 8, pltpu.roll(vec32, 24 * r, 1), 0.0)
-    b_in_row = pltpu.roll(vec32, 96 * (r % 8), 1)[8:9]
+    placed = jnp.where(row < 8, pltpu.roll(vec32[...], 24 * r, 1), 0.0)
+    b_in_row = pltpu.roll(vec32[...], 96 * (r % 8), 1)[8:9]
     placed = placed + jnp.where(row == 8 + r // 8, b_in_row, 0.0)
     sm0[...] = placed.astype(bf16)
-    c_sm = [send(sm0, smr.at[m - 1], mate(m)) for m in (1, 2, 3)]
-
-    def in_cols(j):
-        return wi.at[:, pl.ds(pl.multiple_of(768 * j, 768), 768)]
+    c_sm = share(sm0, smr, mates)
+
+    def in_cols(ref, j):
+        return ref.at[:, pl.ds(pl.multiple_of(768 * j, 768), 768)]
 
     si[q] = wi[:, pl.ds(pl.multiple_of(768 * q, 768), 768)]
-    c_si = [send(in_cols(mate_q(m)), si.at[q], mate(m)) for m in (1, 2, 3)]
-    c_so = send(wo, so, cross, stays)
-    c_sb = send(wb, sb, cross, stays)
-
-    def own_rows(b, zz=None):
-        zz = z if zz is None else zz
+    c_si = send(
+        *[(in_cols(wi, mate_q(m)), si.at[q], mate(m)) for m in (1, 2, 3)], size=si.at[pl.ds(0, 3)]
+    )
+    c_sb = swap(wb, sb, cross, stays)
+
+    def own_rows(b, zz):
         return pl.ds(pl.multiple_of(384 * b + 192 * c + 48 * zz, 16), 48)
 
     def core_rows(b, cc):
         return pl.ds(pl.multiple_of(384 * b + 192 * cc, 16), 192)
 
-    def bundle(landed, full):
+    def b_rows(b, zz, cc):
+        return pl.ds(pl.multiple_of(96 * (2 * zz + cc), 96), 96)
+
+    def bundle(arrived, full):
         for b in range(2):
-            full[own_rows(b), :] = jnp.concatenate([landed[2 * b], landed[2 * b + 1]], axis=0)
-        return [
-            send(full.at[own_rows(b), :], full.at[own_rows(b), :], plane(dz))
-            for dz in (1, 2, 3)
-            for b in range(2)
-        ]
-
-    all_in(c_sa)
-    c_za = bundle(sa, wa_f)
-
-    all_in(c_sm)
-    total = sm0[...].astype(f32) + smr[0].astype(f32) + smr[1].astype(f32) + smr[2].astype(f32)
-    sm1[...] = total.astype(bf16)
-    c_smz = [send(sm1, smz.at[dz - 1], plane(dz)) for dz in (1, 2, 3)]
-
-    arrived(c_tok, alone)
-    xg[q] = xr[...]
-    c_xg = gather(xg)
-
-    all_in(c_smz)
-    total = sm1[...].astype(f32) + smz[0].astype(f32) + smz[1].astype(f32) + smz[2].astype(f32)
-    sm2[...] = total.astype(bf16)
-    c_sms = send(sm2, sms, sibling)
-
-    all_in(c_za)
-    c_ca = [
-        send(wa_f.at[core_rows(b, c), :], wa_f.at[core_rows(b, c), :], sibling) for b in range(2)
-    ]
-
-    arrived(c_so, stays)
-    slot_o = 2 * z + c
-    wo8[slot_o] = so[...]
-    c_zo = [send(wo8.at[slot_o], wo8.at[slot_o], plane(dz)) for dz in (1, 2, 3)]
-    all_in(c_si)
-    c_zi = bundle(si, wi_f)
-    arrived(c_sb, stays)
-
-    def b_rows(zz, cc):
-        return pl.ds(pl.multiple_of(96 * (2 * zz + cc), 96), 96)
-
-    wb_f[b_rows(z, c), :] = sb[...]
-    c_zb = [send(wb_f.at[b_rows(z, c), :], wb_f.at[b_rows(z, c), :], plane(dz)) for dz in (1, 2, 3)]
-    c_cot = send(cot, cr, partner, alone)
-
-    arrived(c_sms)
-    vf[...] = sm2[...].astype(f32) + sms[...].astype(f32)
+            full[own_rows(b, z), :] = jnp.concatenate([arrived[2 * b], arrived[2 * b + 1]], axis=0)
+
+    def rows_a(zz):
+        return [wa_f.at[own_rows(b, zz), :] for b in range(2)]
+
+    def rows_i(zz):
+        return [wi_f.at[own_rows(b, zz), :] for b in range(2)]
+
+    def rows_b(zz):
+        return [wb_f.at[b_rows(0, zz, c), :]]
+
+    def rows_o(zz):
+        return [wo_b.at[16 * c + 4 * q + zz]]
+
+    size_a, size_i = wa_f.at[pl.ds(0, 96), :], wi_f.at[pl.ds(0, 96), :]
+
+    c_sa.landed()
+    bundle(sa, wa_f)
+    c_za = spread(rows_a, size_a)
+
+    c_sm.landed()
+    sm1[...] = wide(sm0[...], smr[0], smr[1], smr[2]).astype(bf16)
+    c_smz = share(sm1, smz, planes)
+
+    c_xg = []
+    for h, rows in enumerate(halves):
+        c_tok[h].landed()
+        xg[q, rows, :] = xr[rows, :]
+        c_xg.append([send((xg.at[q, rows, :], xg.at[q, rows, :], to)) for to in mates])
+
+    c_smz.landed()
+    sm2[...] = wide(sm1[...], smz[0], smz[1], smz[2]).astype(bf16)
+    c_sms = send((sm2, sms, sibling))
+
+    c_za = spread_on(c_za, rows_a, size_a)
+    wo_b[16 * c + 4 * q + z] = wo[...]
+    c_zo = spread(rows_o, None)
+    landed(c_za)
+    c_ca = send(
+        *[(wa_f.at[core_rows(b, c), :], wa_f.at[core_rows(b, c), :], sibling) for b in range(2)],
+        size=wa_f.at[pl.ds(0, 384), :],
+    )
+
+    c_si.landed()
+    bundle(si, wi_f)
+    c_zi = spread(rows_i, size_i)
+    c_sb.landed()
+    wb_f[b_rows(0, z, c), :] = sb[...]
+    c_zb = spread(rows_b, None)
+    c_zo = spread_on(c_zo, rows_o, None)
+
+    c_sms.landed()
+    vf[...] = wide(sm2[...], sms[...])
     b_out, gain1, shift1 = vf[2:3], vf[3:4], vf[4:5]
     b_back, gain2, shift2 = vf[5:6], vf[6:7], vf[7:8]
     turned = pltpu.roll(vf[...], lax.rem(768 - 192 * q, 768), 1)
     b_qkv = jnp.concatenate(
         [turned[0:1, :192], jnp.zeros((1, 192), f32), turned[1:2, :192]], axis=1
     )
-    row1 = lax.broadcasted_iota(jnp.int32, (16, 768), 0)
-    b_in = jnp.sum(jnp.where(row1 == 8 + q, vf[...], 0.0), axis=0, keepdims=True)
-
-    all_in(c_ca)
+    b_in = jnp.sum(jnp.where(row == 8 + q, vf[...], 0.0), axis=0, keepdims=True)
+
+    c_ca.landed()
     c_kv = []
     for m in range(4):
         j = mate_q(m)
         if m:
-            c_xg[m - 1].wait_recv()
+            for copies in c_xg:
+                copies[m - 1].landed()
         out = dot(xg[j], wa_f[...]) + b_qkv
         rows = pl.ds(pl.multiple_of(128 * j, 128), 128)
         qs[rows, :] = (out[:, :192].astype(bf16).astype(f32) * 0.125).astype(bf16)
         kv[c, rows, :] = out[:, 192:].astype(bf16)
-        c_kv.append(send(kv.at[c, rows, :], kv.at[c, rows, :], sibling))
+        c_kv.append(send((kv.at[c, rows, :], kv.at[c, rows, :], sibling)))
+
+    landed(c_zo)
+    chip_o = pl.ds(pl.multiple_of(16 * c + 4 * q, 4), 4)
+    core_o = pl.ds(pl.multiple_of(16 * c, 16), 16)
+    c_po = send(
+        *[(wo_b.at[chip_o], wo_b.at[chip_o], to) for to in mates], size=wo_b.at[pl.ds(0, 12)]
+    )
+    c_zi = spread_on(c_zi, rows_i, size_i)
 
     mt[...] = jnp.zeros_like(mt)
     tot[...] = jnp.zeros_like(tot)
 
-    def expo_rows(h, half, part):
-        return slice(1024 * h + 512 * half + 256 * part, 1024 * h + 512 * half + 256 * part + 256)
+    def expo_rows(h, slot, part):
+        return slice(1024 * h + 512 * slot + 256 * part, 1024 * h + 512 * slot + 256 * part + 256)
 
     def forward_chunk(half, slot, part):
         rows = slice(256 * part, 256 * part + 256)
@@ -251,32 +365,27 @@
 
     forward_chunk(c, 0, 0)
     forward_chunk(c, 0, 1)
-    all_in(c_kv)
+    c_zb = spread_on(c_zb, rows_b, None)
+    landed(c_kv)
     forward_chunk(1 - c, 1, 0)
     forward_chunk(1 - c, 1, 1)
     for h in range(3):
         part = slice(64 * h, 64 * h + 64)
         mt[part, :] = mt[part, :] / tot[h:h + 1, :]
-    mx[...] = jnp.transpose(mt[...]).astype(bf16)
-
-    all_in(c_zo)
-    c_co = [send(wo8.at[2 * zz + c], wo8.at[2 * zz + c], sibling) for zz in range(4)]
-    all_in(c_co)
-    for j in range(8):
-        wo_f[24 * j:24 * j + 24, :] = wo8[j]
-
-    def project(m, _):
-        j = mate_q(m)
-        rows = pl.ds(pl.multiple_of(128 * j, 128), 128)
-        po[j] = dot(mx[rows, :], wo_f[...]).astype(bf16)
-        return 0
-
-    lax.fori_loop(1, 4, project, 0)
-    c_ro = scatter(po, 0, ro.at[0])
-    own = pl.ds(pl.multiple_of(128 * q, 128), 128)
-    attn = dot(mx[own, :], wo_f[...]) + b_out
-    all_in(c_ro)
-    attn = attn + ro[0, 0].astype(f32) + ro[0, 1].astype(f32) + ro[0, 2].astype(f32)
+    for j in range(4):
+        mxs[j] = mt[:, 128 * j:128 * j + 128].astype(bf16)
+    mix[q] = mxs[q]
+    c_mix = to_mates(mxs, mix)
+
+    c_po.landed()
+    c_co = send((wo_b.at[core_o], wo_b.at[core_o], sibling))
+    c_cot = swap(cot, cr, partner, alone)
+    c_co.landed()
+    for b in range(32):
+        wo_f[24 * b:24 * b + 24, :] = wo_b[ORDER[b]]
+    c_mix.landed()
+    mixed = mix[...].reshape(768, 128)
+    attn = dot(mixed, wo_f[...], 0, 0) + b_out
     x32 = xr[...].astype(f32)
     stream = x32 + attn
     squares_x = jnp.sum(x32 * x32)
@@ -289,14 +398,18 @@
     hg[q] = hidden.astype(bf16)
     c_hg = gather(hg)
 
-    all_in(c_zi)
-    c_ci = [
-        send(wi_f.at[core_rows(b, c), :], wi_f.at[core_rows(b, c), :], sibling) for b in range(2)
-    ]
-    all_in(c_zb)
-    c_cb = [send(wb_f.at[b_rows(zz, c), :], wb_f.at[b_rows(zz, c), :], sibling) for zz in range(4)]
-    all_in(c_ci)
-    all_in(c_cb)
+    landed(c_zi)
+    c_ci = send(
+        *[(wi_f.at[core_rows(b, c), :], wi_f.at[core_rows(b, c), :], sibling) for b in range(2)],
+        size=wi_f.at[pl.ds(0, 384), :],
+    )
+    landed(c_zb)
+    c_cb = send(
+        *[(wb_f.at[b_rows(0, zz, c), :], wb_f.at[b_rows(0, zz, c), :], sibling) for zz in range(4)],
+        size=wb_f.at[pl.ds(0, 384), :],
+    )
+    c_ci.landed()
+    c_cb.landed()
 
     def ffn(j):
         pre = dot(hg[j], wi_f[...]) + b_in
@@ -308,15 +421,15 @@
     own_part = ffn(q)
     c_ffn = []
     for m in (1, 2, 3):
-        c_hg[m - 1].wait_recv()
+        c_hg[m - 1].landed()
         j = mate_q(m)
-        po[4 + j] = ffn(j).astype(bf16)
-        c_ffn.append(send(po.at[4 + j], ro.at[1, m - 1], mate(m)))
-    all_in(c_ffn)
-    out = own_part + b_back + ro[1, 0].astype(f32) + ro[1, 1].astype(f32) + ro[1, 2].astype(f32)
+        po[j] = ffn(j).astype(bf16)
+        c_ffn.append(send((po.at[j], ro.at[m - 1], mate(m))))
+    landed(c_ffn)
+    out = own_part + b_back + wide(ro[0], ro[1], ro[2])
     scaled2, inverse2 = norm_parts(hid[...] + out)
-    igs[0] = (scaled2 * gain2 + shift2).astype(bf16)
-    arrived(c_cot, alone)
+    los[...] = (scaled2 * gain2 + shift2).astype(bf16)
+    c_cot.landed()
     dy = cr[...].astype(f32)
     gain2_grad = jnp.sum(dy * scaled2, axis=0, keepdims=True)
     shift2_grad = jnp.sum(dy, axis=0, keepdims=True)
@@ -326,7 +439,7 @@
     dg[q] = low
     back_grad = jnp.sum(low.astype(f32), axis=0, keepdims=True)
     c_dg = gather(dg)
-    c_lo = send(igs.at[0], lo_out, partner, alone)
+    c_lo = swap(los, lo_out, partner, alone)
 
     def ffn_back(j):
         dact = dot(dg[j], wb_f[...], 1, 1)
@@ -336,10 +449,10 @@
     own_part = ffn_back(q)
     c_dh = []
     for m in (1, 2, 3):
-        c_dg[m - 1].wait_recv()
+        c_dg[m - 1].landed()
         j = mate_q(m)
-        po[8 + j] = ffn_back(j).astype(bf16)
-        c_dh.append(send(po.at[8 + j], ro.at[2, m - 1], mate(m)))
+        po[4 + j] = ffn_back(j).astype(bf16)
+        c_dh.append(send((po.at[4 + j], ro.at[2 + m], mate(m))))
 
     def weight_grad(left, right, out, low, rows):
         for i in range(rows // 256):
@@ -352,61 +465,59 @@
         return ref[...].reshape(512, ref.shape[-1])
 
     weight_grad(flat(act), flat(dg), gb, gb_b, 768)
-    c_rb = [send(gb_b.at[b_rows(zz, 1 - c), :], rb.at[zz], sibling) for zz in range(4)]
+    c_rb = send(
+        *[(gb_b.at[b_rows(0, zz, 1 - c), :], rb.at[zz], sibling) for zz in range(4)], size=rb
+    )
     weight_grad(flat(hg), flat(dp), gi, gi_b, 768)
-    c_ri = [send(gi_b.at[core_rows(b, 1 - c), :], ri.at[b], sibling) for b in range(2)]
+    c_ri = send(
+        *[(gi_b.at[core_rows(b, 1 - c), :], ri.at[b], sibling) for b in range(2)], size=ri
+    )
     in_grad = jnp.sum(flat(dp).astype(f32), axis=0, keepdims=True)
 
-    all_in(c_dh)
-    dhidden = (
-        ds2[...] + own_part + ro[2, 0].astype(f32) + ro[2, 1].astype(f32) + ro[2, 2].astype(f32)
-    )
+    def row_sums(copy, mine, theirs, low, landing):
+        copy.landed()
+        for zz in range(4):
+            low[zz] = wide(mine[b_rows(0, zz, c), :], theirs[zz]).astype(bf16)
+        return collect(low, landing)
+
+    def col_sums(copy, mine, theirs, low, landing):
+        copy.landed()
+        for zz in range(4):
+            for b in range(2):
+                part = wide(mine[own_rows(b, zz), :], theirs[b, 48 * zz:48 * zz + 48, :])
+                low[zz, 48 * b:48 * b + 48, :] = part.astype(bf16)
+        return collect(low, landing)
+
+    c_zgb = row_sums(c_rb, gb, rb, s_b, zb)
+    c_zgi = col_sums(c_ri, gi, ri, s_i, zi)
+
+    landed(c_dh)
+    dhidden = ds2[...] + own_part + wide(ro[3], ro[4], ro[5])
     gain1_grad = jnp.sum(dhidden * xh1[...], axis=0, keepdims=True)
     shift1_grad = jnp.sum(dhidden, axis=0, keepdims=True)
     dsum1 = norm_back(dhidden, xh1[...], iv1[:, :1], gain1)
     ds1[...] = dsum1
     low = dsum1.astype(bf16)
-    tg[q] = low
+    da[...] = low
     out_grad = jnp.sum(low.astype(f32), axis=0, keepdims=True)
-    c_tg = gather(tg)
-
-    def row_sums(c_in, partial_sum, recv, low, landing):
-        all_in(c_in)
-        copies = []
-        for zz in range(4):
-            rows = b_rows(zz, c)
-            low[zz] = (partial_sum[rows, :] + recv[zz].astype(f32)).astype(bf16)
-        for dz in (1, 2, 3):
-            copies.append(send(low.at[(z + dz) % 4], landing.at[dz - 1], plane(dz)))
-        return copies
-
-    def col_sums(c_in, partial_sum, recv, low, landing):
-        all_in(c_in)
-        for zz in range(4):
-            for b in range(2):
-                mine = partial_sum[own_rows(b, zz), :]
-                theirs = recv[b, 48 * zz:48 * zz + 48, :].astype(f32)
-                low[zz, b] = (mine + theirs).astype(bf16)
-        return [send(low.at[(z + dz) % 4], landing.at[dz - 1], plane(dz)) for dz in (1, 2, 3)]
-
-    c_zgb = row_sums(c_rb, gb, rb, s_b, zb)
-    c_zgi = col_sums(c_ri, gi, ri, s_i, zi)
-
-    def mixed_back(j):
-        cols = pl.ds(pl.multiple_of(128 * j, 128), 128)
-        dmt[:, cols] = dot(wo_f[...], tg[j], 1, 1)
-
-    mixed_back(q)
-    for m in (1, 2, 3):
-        c_tg[m - 1].wait_recv()
-        mixed_back(mate_q(m))
-    part = dot(mt[...].astype(bf16), flat(tg))
-    for j in range(8):
-        go[j] = part[24 * j:24 * j + 24]
-        go_b[j] = part[24 * j:24 * j + 24].astype(bf16)
-    c_rgo = [send(go_b.at[2 * zz + 1 - c], r_o.at[zz], sibling) for zz in range(4)]
-
+    dmixed_t = dot(wo_f[...], da[...], 1, 1)
+    for j in range(4):
+        dms[j] = dmixed_t[192 * j:192 * j + 192].astype(bf16)
+    dmi[q] = dms[q]
+    c_dm = to_mates(dms, dmi)
+    c_zgb = collect_on(c_zgb, s_b, zb)
+
+    part = dot(mix[...].reshape(768, 128), da[...])
+    for b in range(32):
+        go_b[ORDER[b]] = part[24 * b:24 * b + 24].astype(bf16)
+    other_o = pl.ds(pl.multiple_of(16 * (1 - c), 16), 16)
+    c_rgo = send((go_b.at[other_o], r_o, sibling))
+
+    c_dm.landed()
+    for j in range(4):
+        dmt[:, 128 * j:128 * j + 128] = dmi[j].astype(f32)
     dqt[...] = jnp.zeros_like(dqt)
+    c_zgi = collect_on(c_zgi, s_i, zi)
 
     def backward_chunk(half, slot, part):
         rows = slice(256 * part, 256 * part + 256)
@@ -431,25 +542,37 @@
 
     backward_chunk(1 - c, 1, 0)
     backward_chunk(1 - c, 1, 1)
-    c_dkv = send(dkv.at[1 - c], kvr, sibling)
+    c_dkv = send((dkv.at[1 - c], kvr, sibling))
+    c_rgo.landed()
+    for i in range(16):
+        s_o[i] = wide(go_b[16 * c + i], r_o[i]).astype(bf16)
+    c_pgo = send(
+        *[(s_o.at[pl.ds(4 * mate_q(m), 4)], p_o.at[m - 1], mate(m)) for m in (1, 2, 3)], size=p_o
+    )
     backward_chunk(c, 0, 0)
     backward_chunk(c, 0, 1)
     dall[:, :192] = jnp.transpose(dqt[...] * 0.125).astype(bf16)
-    arrived(c_dkv)
+    c_dkv.landed()
     dall[:, 192:] = (dkv[c] + kvr[...]).astype(bf16)
 
-    def input_back(m, _):
+    own = pl.ds(pl.multiple_of(128 * q, 128), 128)
+    for m in (1, 2, 3):
         j = mate_q(m)
         rows = pl.ds(pl.multiple_of(128 * j, 128), 128)
-        po[12 + j] = dot(dall[rows, :], wa_f[...], 1, 1).astype(bf16)
-        return 0
-
-    lax.fori_loop(1, 4, input_back, 0)
-    c_dx = scatter(po, 12, ro.at[3])
-    own_part = dot(dall[own, :], wa_f[...], 1, 1)
+        po[8 + j] = dot(dall[rows, :], wa_f[...], 1, 1).astype(bf16)
+    c_dx = [
+        send(
+            *[(po.at[8 + mate_q(m), rows, :], ro.at[5 + m, rows, :], mate(m)) for m in (1, 2, 3)],
+            size=ro.at[pl.ds(6, 3), rows, :],
+        )
+        for rows in halves
+    ]
+    ds1[...] += dot(dall[own, :], wa_f[...], 1, 1)
 
     weight_grad(flat(xg), dall[...], ga, ga_b, 768)
-    c_rga = [send(ga_b.at[core_rows(b, 1 - c), :], ra.at[b], sibling) for b in range(2)]
+    c_rga = send(
+        *[(ga_b.at[core_rows(b, 1 - c), :], ra.at[b], sibling) for b in range(2)], size=ra
+    )
     sums = jnp.sum(dall[...].astype(f32), axis=0, keepdims=True)
 
     rest = jnp.zeros((1, 576), f32)
@@ -458,7 +581,6 @@
          jnp.concatenate([sums[:, 384:], rest], axis=1),
          jnp.zeros((6, 768), f32)], axis=0,
     )
-    gs0[...] = jnp.zeros_like(gs0)
     gs0[0:8, :] = pltpu.roll(head_rows, 192 * q, 1)
     gs0[2:3, :] = out_grad
     gs0[3:4, :] = gain1_grad
@@ -472,170 +594,166 @@
         + jnp.where(row2 == 4, squares_x, 0.0)
         + jnp.where(row2 == 5, squares_s, 0.0)
     )
-    c_gs = [send(gs0, gsr.at[m - 1], mate(m)) for m in (1, 2, 3)]
-
-    all_in(c_rgo)
-    for zz in range(4):
-        s_o[zz] = (go[2 * zz + c] + r_o[zz].astype(f32)).astype(bf16)
-    c_zgo = [send(s_o.at[(z + dz) % 4], z_o.at[dz - 1], plane(dz)) for dz in (1, 2, 3)]
+    c_gs = share(gs0, gsr, mates)
+
     c_zga = col_sums(c_rga, ga, ra, s_a, za)
-
-    all_in(c_dx)
-    input_grad = (
-        ds1[...] + own_part + ro[3, 0].astype(f32) + ro[3, 1].astype(f32) + ro[3, 2].astype(f32)
-    )
-    igs[1] = input_grad.astype(bf16)
-    c_ig = send(igs.at[1], igr, partner, alone)
-
-    all_in(c_gs)
+    c_pgo.landed()
+    for i in range(4):
+        t_o[i] = wide(s_o[4 * q + i], p_o[0, i], p_o[1, i], p_o[2, i]).astype(bf16)
+    c_zgo = collect(t_o, z_o)
+
+    c_ig = []
+    for h, rows in enumerate(halves):
+        c_dx[h].landed()
+        grad = ds1[rows, :] + wide(ro[6, rows, :], ro[7, rows, :], ro[8, rows, :])
+        igs[rows, :] = grad.astype(bf16)
+        c_ig.append(swap(igs.at[rows, :], igr.at[rows, :], partner, alone))
+
+    c_zga = collect_on(c_zga, s_a, za)
+    c_zgo = collect_on(c_zgo, t_o, z_o)
+    c_gs.landed()
     gs1[...] = gs0[...] + gsr[0] + gsr[1] + gsr[2]
-    c_gsz = [send(gs1, gsz.at[dz - 1], plane(dz)) for dz in (1, 2, 3)]
-
-    all_in(c_zgb)
-    fb[...] = (
-        s_b[z].astype(f32) + zb[0].astype(f32) + zb[1].astype(f32) + zb[2].astype(f32)
-    )
-    c_fb = send(fb, db_out, cross, stays)
-
-    def col_final(c_in, low, landing, out):
-        all_in(c_in)
-        for b in range(2):
-            whole = (
-                low[z, b].astype(f32) + landing[0, b].astype(f32)
-                + landing[1, b].astype(f32) + landing[2, b].astype(f32)
-            )
-            out[2 * b] = whole[:24]
-            out[2 * b + 1] = whole[24:]
+    c_gsz = share(gs1, gsz, planes)
+
+    landed(c_zgb)
+    fb[...] = wide(s_b[z], zb[0], zb[1], zb[2]).astype(bf16)
+    c_fb = swap(fb, db_out, cross, stays)
+
+    def col_final(copies, low, landing, out):
+        landed(copies)
+        for i in range(4):
+            rows = slice(24 * i, 24 * i + 24)
+            out[i] = wide(
+                low[z, rows, :], landing[0, rows, :], landing[1, rows, :], landing[2, rows, :]
+            ).astype(bf16)
 
     col_final(c_zgi, s_i, zi, fi)
-
-    def out_cols(j):
-        return di_out.at[:, pl.ds(pl.multiple_of(768 * j, 768), 768)]
-
-    c_fi = [send(fi.at[mate_q(m)], out_cols(q), mate(m)) for m in (1, 2, 3)]
+    c_fi = send(
+        *[(fi.at[mate_q(m)], in_cols(di_out, q), mate(m)) for m in (1, 2, 3)],
+        size=fi.at[pl.ds(0, 3)],
+    )
     di_out[:, pl.ds(pl.multiple_of(768 * q, 768), 768)] = fi[q]
-
-    all_in(c_zgo)
-    fo[...] = (
-        s_o[z].astype(f32) + z_o[0].astype(f32) + z_o[1].astype(f32) + z_o[2].astype(f32)
-    )
-    c_fo = send(fo, do_out, cross, stays)
-
-    all_in(c_gsz)
-    gs2[...] = gs1[...] + gsz[0] + gsz[1] + gsz[2]
-    c_gss = send(gs2, gss, sibling)
 
     col_final(c_zga, s_a, za, fa)
     la[q] = fa[q]
-    c_fa = [send(fa.at[mate_q(m)], la.at[q], mate(m)) for m in (1, 2, 3)]
-
-    arrived(c_ig, alone)
-    ig_out[...] = igr[...].astype(f32)
-
-    arrived(c_gss)
+    c_fa = to_mates(fa, la)
+
+    landed(c_zgo)
+    do_out[...] = wide(t_o[z], z_o[0], z_o[1], z_o[2])
+
+    c_gsz.landed()
+    gs2[...] = gs1[...] + gsz[0] + gsz[1] + gsz[2]
+    c_gss = send((gs2, gss, sibling))
+    c_gss.landed()
     whole = gs2[...] + gss[...]
     sm_out[0:8, :] = pltpu.roll(whole, lax.rem(768 - 24 * r, 768), 1)[:8, :128]
-    mine = jnp.sum(
-        jnp.where(lax.broadcasted_iota(jnp.int32, (16, 768), 0) == 8 + r // 8, whole, 0.0),
-        axis=0, keepdims=True,
-    )
+    mine = jnp.sum(jnp.where(row == 8 + r // 8, whole, 0.0), axis=0, keepdims=True)
     mine = pltpu.roll(jnp.broadcast_to(mine, (8, 768)), lax.rem(768 - 96 * (r % 8), 768), 1)
     row3 = lax.broadcasted_iota(jnp.int32, (8, 128), 0)
     sm_out[8:16, :] = jnp.where(row3 < 4, mine[:, :128], whole[8:16, :128])
 
-    all_in(c_fa)
+    c_lo.landed()
+    c_fb.landed()
+    c_fi.landed()
+    c_fa.landed()
+    landed(c_ig)
+    assert len(sends) == COPIES, len(sends)
+    for copy in sends:
+        copy.left()
+
+
+def finish_kernel(
+    lo, ig, la, do, di, db, sm,
+    lo_out, ig_out, dq_out, dk_out, dv_out, do_out, bq, bv, bo, g1, s1, di_out, bi, db_out, bb,
+    g2, s2, rms_out,
+):
+    lo_out[...] = lo[...]
+    ig_out[...] = ig[...].astype(f32)
     for j in range(4):
         cols = slice(192 * j, 192 * j + 192)
-        dq_out[:, cols] = la[j, :, :192]
-        dk_out[:, cols] = la[j, :, 192:384]
-        dv_out[:, cols] = la[j, :, 384:]
-
-    arrived(c_lo, alone)
-    arrived(c_fb, stays)
-    arrived(c_fo, stays)
-    all_in(c_fi)
-    for cp, own_copy in sends:
-        if own_copy is None:
-            cp.wait_send()
-        else:
-            @pl.when(jnp.logical_not(own_copy))
-            def _():
-                cp.wait_send()
-
-
-COPIES = 200
+        dq_out[:, cols] = la[j, :, :192].astype(f32)
+        dk_out[:, cols] = la[j, :, 192:384].astype(f32)
+        dv_out[:, cols] = la[j, :, 384:].astype(f32)
+    do_out[...] = do[...]
+    di_out[...] = di[...].astype(f32)
+    db_out[...] = db[...].astype(f32)
+    for i, out in enumerate((bq, bv, bo, g1, s1, bb, g2, s2)):
+        out[...] = sm[i:i + 1, :24]
+    bi[...] = sm[8:9, :96]
+    lane = lax.broadcasted_iota(jnp.int32, (1, 128), 1)
+    means = jnp.where(lane == 0, sm[12:13, :], sm[13:14, :]) / (4096 * 768)
+    rms_out[...] = jnp.sqrt(means)[:, :2]
 
 
 def fused(
     tokens, w_query, w_key, w_value, w_out, b_query, b_value, b_out, norm1_gain, norm1_shift,
     w_in, b_in, w_back, b_back, norm2_gain, norm2_shift, cotangent,
 ):
-    vectors = jnp.stack(
-        [b_query, b_value, b_out, norm1_gain, norm1_shift, b_back, norm2_gain, norm2_shift]
-    )
-    vec = jnp.concatenate(
-        [
-            jnp.pad(vectors, ((0, 0), (0, 768 - 24))),
-            jnp.pad(b_in[None, :], ((0, 7), (0, 768 - 96))),
-        ],
-        axis=0,
+    vectors = (
+        b_query, b_value, b_out, norm1_gain, norm1_shift, b_back, norm2_gain, norm2_shift, b_in
     )
     vm = pl.BlockSpec(memory_space=pltpu.VMEM)
 
     def v(*shape, t=bf16):
         return pltpu.VMEM(shape, t)
 
-    outs = (
-        jax.ShapeDtypeStruct((128, 768), bf16),
-        jax.ShapeDtypeStruct((128, 768), f32),
-        jax.ShapeDtypeStruct((24, 768), f32),
-        jax.ShapeDtypeStruct((24, 768), f32),
-        jax.ShapeDtypeStruct((24, 768), f32),
-        jax.ShapeDtypeStruct((24, 768), f32),
-        jax.ShapeDtypeStruct((24, 3072), f32),
-        jax.ShapeDtypeStruct((96, 768), f32),
-        jax.ShapeDtypeStruct((16, 128), f32),
-    )
+    def s(*shape, t=f32):
+        return jax.ShapeDtypeStruct(shape, t)
+
     scratch = [
         v(128, 768), v(128, 768), v(4, 128, 768), v(4, 24, 576), v(4, 24, 576), v(4, 24, 768),
-        v(96, 768), v(24, 768), v(768, 576), v(768, 768), v(768, 768), v(8, 24, 768), v(192, 768),
+        v(96, 768), v(768, 576), v(768, 768), v(768, 768), v(32, 24, 768), v(768, 768),
+        v(16, 768, t=f32),
         v(16, 768), v(3, 16, 768), v(16, 768), v(3, 16, 768), v(16, 768), v(16, 768),
         v(16, 768, t=f32),
         v(512, 192), v(2, 512, 384), v(3072, 512), v(192, 512, t=f32), v(8, 512, t=f32),
-        v(512, 192), v(16, 128, 768), v(4, 3, 128, 768),
+        v(4, 192, 128), v(4, 192, 128), v(12, 128, 768), v(9, 128, 768),
         v(128, 768, t=f32), v(128, 768, t=f32), v(128, 128, t=f32), v(4, 128, 768),
         v(4, 128, 768, t=f32), v(4, 128, 768), v(128, 768, t=f32), v(4, 128, 768),
-        v(4, 128, 768), v(4, 128, 768), v(192, 512, t=f32), v(192, 512, t=f32),
-        v(2, 512, 384, t=f32), v(512, 384, t=f32), v(512, 576), v(128, 768, t=f32),
-        v(768, 576, t=f32), v(768, 576), v(2, 192, 576), v(4, 2, 48, 576), v(3, 2, 48, 576),
-        v(4, 24, 576, t=f32), v(4, 24, 576, t=f32),
-        v(768, 768, t=f32), v(768, 768), v(2, 192, 768), v(4, 2, 48, 768), v(3, 2, 48, 768),
-        v(4, 24, 768, t=f32),
-        v(768, 768, t=f32), v(768, 768), v(4, 96, 768), v(4, 96, 768), v(3, 96, 768),
-        v(96, 768, t=f32),
-        v(8, 24, 768, t=f32), v(8, 24, 768), v(4, 24, 768), v(4, 24, 768), v(3, 24, 768),
-        v(24, 768, t=f32),
-        v(2, 128, 768), v(128, 768), v(16, 768, t=f32), v(3, 16, 768, t=f32),
+        v(4, 128, 768), v(128, 768), v(4, 192, 128), v(4, 192, 128),
+        v(192, 512, t=f32), v(192, 512, t=f32), v(2, 512, 384, t=f32), v(512, 384, t=f32),
+        v(512, 576), v(128, 768, t=f32),
+        v(768, 576, t=f32), v(768, 576), v(2, 192, 576), v(4, 96, 576), v(4, 96, 576),
+        v(4, 24, 576),
+        v(768, 768, t=f32), v(768, 768), v(2, 192, 768), v(4, 96, 768), v(4, 96, 768),
+        v(4, 24, 768),
+        v(768, 768, t=f32), v(768, 768), v(4, 96, 768), v(4, 96, 768), v(4, 96, 768),
+        v(96, 768),
+        v(32, 24, 768), v(16, 24, 768), v(16, 24, 768), v(3, 4, 24, 768), v(4, 24, 768),
+        v(4, 24, 768),
+        v(128, 768), v(128, 768), v(16, 768, t=f32), v(3, 16, 768, t=f32),
         v(16, 768, t=f32), v(3, 16, 768, t=f32), v(16, 768, t=f32), v(16, 768, t=f32),
         pltpu.SemaphoreType.DMA((COPIES,)), pltpu.SemaphoreType.DMA((COPIES,)),
     ]
-    lo, ig, dq, dk, dv, do, di, db, sm = pl.pallas_call(
+    parts = pl.pallas_call(
         layer_kernel,
-        out_shape=outs,
-        in_specs=[vm] * 9,
-        out_specs=[vm] * 9,
+        out_shape=(
+            s(128, 768, t=bf16), s(128, 768, t=bf16), s(4, 24, 576, t=bf16), s(24, 768),
+            s(24, 3072, t=bf16), s(96, 768, t=bf16), s(16, 128),
+        ),
+        in_specs=[vm] * 17,
+        out_specs=[vm] * 7,
         scratch_shapes=scratch,
         compiler_params=pltpu.CompilerParams(
-            collective_id=0, has_side_effects=True, vmem_limit_bytes=60 << 20
+            collective_id=0, has_side_effects=True, vmem_limit_bytes=58 << 20
         ),
         name="layer",
-    )(tokens, cotangent, w_query, w_key, w_value, w_out, w_in, w_back, vec)
-    small = [sm[i, :24] for i in range(8)]
-    rms = jnp.sqrt(jnp.stack([sm[12, 0], sm[13, 0]]) / (4096 * 768))
-    return (
-        lo, ig, dq, dk, dv, do, small[0], small[1], small[2], small[3], small[4], di, sm[8, :96],
-        db, small[5], small[6], small[7], rms,
-    )
+    )(
+        tokens, cotangent, w_query, w_key, w_value, w_out, w_in, w_back,
+        *[vector.reshape(1, -1) for vector in vectors],
+    )
+    square, small = s(24, 768), s(1, 24)
+    outs = pl.pallas_call(
+        finish_kernel,
+        out_shape=(
+            (s(128, 768, t=bf16), s(128, 768)) + (square,) * 4 + (small,) * 5
+            + (s(24, 3072), s(1, 96), s(96, 768)) + (small,) * 3 + (s(1, 2),)
+        ),
+        in_specs=[vm] * 7,
+        out_specs=[vm] * 18,
+        name="finish",
+    )(*parts)
+    return tuple(o.reshape(o.shape[1:]) if o.shape[0] == 1 else o for o in outs)
 
 
 def normalize(values, gain, shift):

time: 167 us -> 144 us (0.86)
  the two profiles are of different devices: /device:TPU:0 before, /device:TPU:1 now
where the time goes in v2:
time: 144 us; the launch traced here: 143 us
  Pallas kernels  142 us (99%)
    pallas_call x1, Pallas kernels, fused(): pl.pallas_call(layer_kernel, out_shape=(s(128, 768, t=bf16), s(128, 768,...  140 us

profile of v2, /device:TPU:1, one launch (start us, length us, event | category | flops | bytes accessed | tf_op | source)
XLA Modules:
  0.0 143.1 jit_solution(3145517203201374084)
XLA Ops:
  0.7 139.8 %layer.1 = (bf16[128,768]{1,0:T(8,128)(2,1)}, bf16[128,768]{1,0:T(8,128)(2,1)}, bf16[4,24,576]{2,1,0:T(8,128)(2,1)}, f32[24,768]{1,0:T(8,128)}, bf16[24,3072]{1,...) custom-call(bf16[128,768]{1,0:T(8,128)(2,1)} %tok.1, bf16[128,768]{1,0:T(8,128)(2,1)} %cot.1, ...), custom_call_target="tpu_custom_call" | custom-call | tf_op jit(solution)/shard_map/layer/pallas_call | solution.py:728
  140.5 2.5 %finish.1 = (bf16[128,768]{1,0:T(8,128)(2,1)}, f32[128,768]{1,0:T(8,128)}, f32[24,768]{1,0:T(8,128)}, f32[24,768]{1,0:T(8,128)}, f32[24,768]{1,0:T(8,128)}, /*in...) custom-call(bf16[128,768]{1,0:T(8,128)(2,1)} %get-tuple-element.43.l, ...), custom_call_target="tpu_custom_call" | custom-call | tf_op jit(solution)/shard_map/finish/pallas_call | solution.py:746

commit v3 on v2

--- a/solution.py
+++ b/solution.py
@@ -12,7 +12,7 @@
 bf16 = jnp.bfloat16
 DH = 64
 epsilon = 1e-12
-COPIES = 87
+COPIES = 84
 
 
 def dot(a, b, ca=1, cb=0):
@@ -82,14 +82,14 @@
     tok, cot, wq, wk, wv, wo, wi, wb, bq, bv, bo, g1, s1, bb, g2, s2, bi,
     lo_out, igr, la, do_out, di_out, db_out, sm_out,
     xr, cr, xg, pa, sa, si, sb, wa_f, wi_f, wb_f, wo_b, wo_f,
-    vec32, sm0, smr, sm1, smz, sm2, sms, vf,
+    vec32, vecs, vf,
     qs, kv, ee, mt, tot, mxs, mix, po, ro, hid, xh1, iv1, hg, gp, act, ds2, dg, dp, da, dms, dmi,
     dmt, dqt, dkv, kvr, dall, ds1,
     ga, ga_b, ra, s_a, za, fa,
     gi, gi_b, ri, s_i, zi, fi,
     gb, gb_b, rb, s_b, zb, fb,
     go_b, r_o, s_o, p_o, t_o, z_o,
-    los, igs, gs0, gsr, gs1, gsz, gs2, gss,
+    los, igs, gs0, gsb, gsr, gst, gsm, gsu, gsz,
     ssem, rsem,
 ):
     d = lax.axis_index("dp")
@@ -189,6 +189,11 @@
             copy(plane(2), None, None), copy(plane(1), z < 3, z > 0), copy(plane(3), z > 0, z < 3)
         ]
 
+    def spread_all(part, size):
+        return [
+            send(*[(ref, ref, to) for ref in part(z)], size=size) for to in planes
+        ]
+
     def spread_on(copies, part, size):
         copies[0].landed()
         to = dev(x, y, c, lax.rem(3 * (z + 3), 4))
@@ -216,14 +221,25 @@
 
     @pl.when(z == 0)
     def _():
-        for ref in (za, zi, zb, z_o):
+        for ref in (zi, zb, z_o):
             ref[0] = jnp.zeros_like(ref[0])
 
     @pl.when(z == 3)
     def _():
-        for ref in (za, zi, zb, z_o):
+        for ref in (zi, zb, z_o):
             ref[1] = jnp.zeros_like(ref[1])
 
+    vec32[...] = jnp.zeros_like(vec32)
+    for i, ref in enumerate((bq, bv, bo, g1, s1, bb, g2, s2)):
+        vec32[i:i + 1, :24] = ref[...].astype(f32)
+    vec32[8:9, :96] = bi[...].astype(f32)
+    slot = 16 * c + 4 * q + z
+    chip_slots = pl.ds(pl.multiple_of(16 * c + 4 * q, 4), 4)
+    core_slots = pl.ds(pl.multiple_of(16 * c, 16), 16)
+    vecs[slot] = vec32[...].astype(bf16)
+    c_vz = send(
+        *[(vecs.at[slot], vecs.at[slot], to) for to in planes], size=vecs.at[pl.ds(0, 3)]
+    )
     halves = [slice(0, 64), slice(64, 128)]
     c_tok = [swap(tok.at[rows, :], xr.at[rows, :], partner, alone) for rows in halves]
     for j in range(4):
@@ -231,16 +247,6 @@
         pa[j] = jnp.concatenate([wq[:, cols], wk[:, cols], wv[:, cols]], axis=1)
     sa[q] = pa[q]
     c_sa = to_mates(pa, sa)
-    vec32[...] = jnp.zeros_like(vec32)
-    for i, ref in enumerate((bq, bv, bo, g1, s1, bb, g2, s2)):
-        vec32[i:i + 1, :24] = ref[...].astype(f32)
-    vec32[8:9, :96] = bi[...].astype(f32)
-    row = lax.broadcasted_iota(jnp.int32, (16, 768), 0)
-    placed = jnp.where(row < 8, pltpu.roll(vec32[...], 24 * r, 1), 0.0)
-    b_in_row = pltpu.roll(vec32[...], 96 * (r % 8), 1)[8:9]
-    placed = placed + jnp.where(row == 8 + r // 8, b_in_row, 0.0)
-    sm0[...] = placed.astype(bf16)
-    c_sm = share(sm0, smr, mates)
 
     def in_cols(ref, j):
         return ref.at[:, pl.ds(pl.multiple_of(768 * j, 768), 768)]
@@ -278,43 +284,40 @@
 
     size_a, size_i = wa_f.at[pl.ds(0, 96), :], wi_f.at[pl.ds(0, 96), :]
 
+    c_vz.landed()
+    gsb[...] = jnp.zeros_like(gsb)
+    c_vm = send(
+        *[(vecs.at[chip_slots], vecs.at[chip_slots], to) for to in mates],
+        size=vecs.at[pl.ds(0, 12)],
+    )
     c_sa.landed()
     bundle(sa, wa_f)
-    c_za = spread(rows_a, size_a)
-
-    c_sm.landed()
-    sm1[...] = wide(sm0[...], smr[0], smr[1], smr[2]).astype(bf16)
-    c_smz = share(sm1, smz, planes)
-
-    c_xg = []
-    for h, rows in enumerate(halves):
-        c_tok[h].landed()
-        xg[q, rows, :] = xr[rows, :]
-        c_xg.append([send((xg.at[q, rows, :], xg.at[q, rows, :], to)) for to in mates])
-
-    c_smz.landed()
-    sm2[...] = wide(sm1[...], smz[0], smz[1], smz[2]).astype(bf16)
-    c_sms = send((sm2, sms, sibling))
-
-    c_za = spread_on(c_za, rows_a, size_a)
-    wo_b[16 * c + 4 * q + z] = wo[...]
-    c_zo = spread(rows_o, None)
-    landed(c_za)
-    c_ca = send(
-        *[(wa_f.at[core_rows(b, c), :], wa_f.at[core_rows(b, c), :], sibling) for b in range(2)],
-        size=wa_f.at[pl.ds(0, 384), :],
-    )
-
+    c_za = spread_all(rows_a, size_a)
+    c_vm.landed()
+    c_vs = send((vecs.at[core_slots], vecs.at[core_slots], sibling))
+    wo_b[slot] = wo[...]
+    c_zo = spread_all(rows_o, None)
     c_si.landed()
     bundle(si, wi_f)
     c_zi = spread(rows_i, size_i)
     c_sb.landed()
     wb_f[b_rows(0, z, c), :] = sb[...]
     c_zb = spread(rows_b, None)
-    c_zo = spread_on(c_zo, rows_o, None)
-
-    c_sms.landed()
-    vf[...] = wide(sm2[...], sms[...])
+    c_xg = []
+    for h, rows in enumerate(halves):
+        c_tok[h].landed()
+        xg[q, rows, :] = xr[rows, :]
+        c_xg.append([send((xg.at[q, rows, :], xg.at[q, rows, :], to)) for to in mates])
+
+    c_vs.landed()
+    every = [vecs[ORDER[b]].astype(f32) for b in range(32)]
+    vf[0:8, :] = jnp.concatenate([part[:8, :24] for part in every], axis=1)
+    for i in range(4):
+        vf[8 + i:9 + i, :] = jnp.concatenate(
+            [part[8:9, :96] for part in every[8 * i:8 * i + 8]], axis=1
+        )
+    vf[12:16, :] = jnp.zeros((4, 768), f32)
+    row = lax.broadcasted_iota(jnp.int32, (16, 768), 0)
     b_out, gain1, shift1 = vf[2:3], vf[3:4], vf[4:5]
     b_back, gain2, shift2 = vf[5:6], vf[6:7], vf[7:8]
     turned = pltpu.roll(vf[...], lax.rem(768 - 192 * q, 768), 1)
@@ -322,6 +325,17 @@
         [turned[0:1, :192], jnp.zeros((1, 192), f32), turned[1:2, :192]], axis=1
     )
     b_in = jnp.sum(jnp.where(row == 8 + q, vf[...], 0.0), axis=0, keepdims=True)
+    landed(c_za)
+    c_ca = send(
+        *[(wa_f.at[core_rows(b, c), :], wa_f.at[core_rows(b, c), :], sibling) for b in range(2)],
+        size=wa_f.at[pl.ds(0, 384), :],
+    )
+
+
+    landed(c_zo)
+    c_po = send(
+        *[(wo_b.at[chip_slots], wo_b.at[chip_slots], to) for to in mates], size=wo_b.at[pl.ds(0, 12)]
+    )
 
     c_ca.landed()
     c_kv = []
@@ -336,13 +350,6 @@
         kv[c, rows, :] = out[:, 192:].astype(bf16)
         c_kv.append(send((kv.at[c, rows, :], kv.at[c, rows, :], sibling)))
 
-    landed(c_zo)
-    chip_o = pl.ds(pl.multiple_of(16 * c + 4 * q, 4), 4)
-    core_o = pl.ds(pl.multiple_of(16 * c, 16), 16)
-    c_po = send(
-        *[(wo_b.at[chip_o], wo_b.at[chip_o], to) for to in mates], size=wo_b.at[pl.ds(0, 12)]
-    )
-    c_zi = spread_on(c_zi, rows_i, size_i)
 
     mt[...] = jnp.zeros_like(mt)
     tot[...] = jnp.zeros_like(tot)
@@ -365,7 +372,8 @@
 
     forward_chunk(c, 0, 0)
     forward_chunk(c, 0, 1)
-    c_zb = spread_on(c_zb, rows_b, None)
+    c_po.landed()
+    c_co = send((wo_b.at[core_slots], wo_b.at[core_slots], sibling))
     landed(c_kv)
     forward_chunk(1 - c, 1, 0)
     forward_chunk(1 - c, 1, 1)
@@ -376,10 +384,8 @@
         mxs[j] = mt[:, 128 * j:128 * j + 128].astype(bf16)
     mix[q] = mxs[q]
     c_mix = to_mates(mxs, mix)
-
-    c_po.landed()
-    c_co = send((wo_b.at[core_o], wo_b.at[core_o], sibling))
-    c_cot = swap(cot, cr, partner, alone)
+    c_zi = spread_on(c_zi, rows_i, size_i)
+
     c_co.landed()
     for b in range(32):
         wo_f[24 * b:24 * b + 24, :] = wo_b[ORDER[b]]
@@ -397,6 +403,8 @@
     hid[...] = hidden
     hg[q] = hidden.astype(bf16)
     c_hg = gather(hg)
+    c_zb = spread_on(c_zb, rows_b, None)
+    c_cot = swap(cot, cr, partner, alone)
 
     landed(c_zi)
     c_ci = send(
@@ -409,21 +417,25 @@
         size=wb_f.at[pl.ds(0, 384), :],
     )
     c_ci.landed()
-    c_cb.landed()
 
     def ffn(j):
         pre = dot(hg[j], wi_f[...]) + b_in
         phi = 0.5 + 0.5 * lax.erf(pre * 0.7071067811865476)
         gp[j] = phi + pre * jnp.exp(-0.5 * pre * pre) * 0.3989422804014327
         act[j] = (pre * phi).astype(bf16)
+
+    def ffn_out(j):
         return dot(act[j], wb_f[...])
 
-    own_part = ffn(q)
+    ffn(q)
+    c_cb.landed()
+    own_part = ffn_out(q)
     c_ffn = []
     for m in (1, 2, 3):
         c_hg[m - 1].landed()
         j = mate_q(m)
-        po[j] = ffn(j).astype(bf16)
+        ffn(j)
+        po[j] = ffn_out(j).astype(bf16)
         c_ffn.append(send((po.at[j], ro.at[m - 1], mate(m))))
     landed(c_ffn)
     out = own_part + b_back + wide(ro[0], ro[1], ro[2])
@@ -480,16 +492,16 @@
             low[zz] = wide(mine[b_rows(0, zz, c), :], theirs[zz]).astype(bf16)
         return collect(low, landing)
 
-    def col_sums(copy, mine, theirs, low, landing):
+    def col_sums(copy, mine, theirs, low):
         copy.landed()
         for zz in range(4):
             for b in range(2):
                 part = wide(mine[own_rows(b, zz), :], theirs[b, 48 * zz:48 * zz + 48, :])
                 low[zz, 48 * b:48 * b + 48, :] = part.astype(bf16)
-        return collect(low, landing)
 
     c_zgb = row_sums(c_rb, gb, rb, s_b, zb)
-    c_zgi = col_sums(c_ri, gi, ri, s_i, zi)
+    col_sums(c_ri, gi, ri, s_i)
+    c_zgi = collect(s_i, zi)
 
     landed(c_dh)
     dhidden = ds2[...] + own_part + wide(ro[3], ro[4], ro[5])
@@ -555,6 +567,48 @@
     c_dkv.landed()
     dall[:, 192:] = (dkv[c] + kvr[...]).astype(bf16)
 
+    sums = jnp.sum(dall[...].astype(f32), axis=0, keepdims=True)
+    rest = jnp.zeros((1, 576), f32)
+    head_rows = jnp.concatenate(
+        [jnp.concatenate([sums[:, :192], rest], axis=1),
+         jnp.concatenate([sums[:, 384:], rest], axis=1),
+         jnp.zeros((6, 768), f32)], axis=0,
+    )
+    gs0[0:8, :] = pltpu.roll(head_rows, 192 * q, 1)
+    gs0[2:3, :] = out_grad
+    gs0[3:4, :] = gain1_grad
+    gs0[4:5, :] = shift1_grad
+    gs0[5:6, :] = back_grad
+    gs0[6:7, :] = gain2_grad
+    gs0[7:8, :] = shift2_grad
+    row2 = lax.broadcasted_iota(jnp.int32, (8, 768), 0)
+    gs0[8:16, :] = (
+        jnp.where(row2 == q, in_grad, 0.0)
+        + jnp.where(row2 == 4, squares_x, 0.0)
+        + jnp.where(row2 == 5, squares_s, 0.0)
+    )
+    for b in range(32):
+        gsb[ORDER[b], 0:8, 0:24] = gs0[0:8, 24 * b:24 * b + 24]
+        at = 96 * (b % 8)
+        gsb[ORDER[b], 8:9, 0:96] = gs0[8 + b // 8:9 + b // 8, at:at + 96]
+        gsb[ORDER[b], 12:14, :] = gs0[12:14, 0:128]
+    other_slots = pl.ds(pl.multiple_of(16 * (1 - c), 16), 16)
+    c_gs = send((gsb.at[other_slots], gsr, sibling))
+    c_pgo.landed()
+    for i in range(4):
+        t_o[i] = wide(s_o[4 * q + i], p_o[0, i], p_o[1, i], p_o[2, i]).astype(bf16)
+    c_zgo = collect(t_o, z_o)
+
+    weight_grad(flat(xg), dall[...], ga, ga_b, 768)
+    c_rga = send(
+        *[(ga_b.at[core_rows(b, 1 - c), :], ra.at[b], sibling) for b in range(2)], size=ra
+    )
+    c_gs.landed()
+    for i in range(16):
+        gst[i] = gsb[16 * c + i] + gsr[i]
+    c_gm = send(
+        *[(gst.at[pl.ds(4 * mate_q(m), 4)], gsm.at[m - 1], mate(m)) for m in (1, 2, 3)], size=gsm
+    )
     own = pl.ds(pl.multiple_of(128 * q, 128), 128)
     for m in (1, 2, 3):
         j = mate_q(m)
@@ -567,53 +621,17 @@
         )
         for rows in halves
     ]
+    col_sums(c_rga, ga, ra, s_a)
+    c_zga = [send((s_a.at[lax.rem(z + 1 + i, 4)], za.at[i], to)) for i, to in enumerate(planes)]
     ds1[...] += dot(dall[own, :], wa_f[...], 1, 1)
 
-    weight_grad(flat(xg), dall[...], ga, ga_b, 768)
-    c_rga = send(
-        *[(ga_b.at[core_rows(b, 1 - c), :], ra.at[b], sibling) for b in range(2)], size=ra
-    )
-    sums = jnp.sum(dall[...].astype(f32), axis=0, keepdims=True)
-
-    rest = jnp.zeros((1, 576), f32)
-    head_rows = jnp.concatenate(
-        [jnp.concatenate([sums[:, :192], rest], axis=1),
-         jnp.concatenate([sums[:, 384:], rest], axis=1),
-         jnp.zeros((6, 768), f32)], axis=0,
-    )
-    gs0[0:8, :] = pltpu.roll(head_rows, 192 * q, 1)
-    gs0[2:3, :] = out_grad
-    gs0[3:4, :] = gain1_grad
-    gs0[4:5, :] = shift1_grad
-    gs0[5:6, :] = back_grad
-    gs0[6:7, :] = gain2_grad
-    gs0[7:8, :] = shift2_grad
-    row2 = lax.broadcasted_iota(jnp.int32, (8, 768), 0)
-    gs0[8:16, :] = (
-        jnp.where(row2 == q, in_grad, 0.0)
-        + jnp.where(row2 == 4, squares_x, 0.0)
-        + jnp.where(row2 == 5, squares_s, 0.0)
-    )
-    c_gs = share(gs0, gsr, mates)
-
-    c_zga = col_sums(c_rga, ga, ra, s_a, za)
-    c_pgo.landed()
+    c_gm.landed()
     for i in range(4):
-        t_o[i] = wide(s_o[4 * q + i], p_o[0, i], p_o[1, i], p_o[2, i]).astype(bf16)
-    c_zgo = collect(t_o, z_o)
-
-    c_ig = []
-    for h, rows in enumerate(halves):
-        c_dx[h].landed()
-        grad = ds1[rows, :] + wide(ro[6, rows, :], ro[7, rows, :], ro[8, rows, :])
-        igs[rows, :] = grad.astype(bf16)
-        c_ig.append(swap(igs.at[rows, :], igr.at[rows, :], partner, alone))
-
-    c_zga = collect_on(c_zga, s_a, za)
+        gsu[i] = gst[4 * q + i] + gsm[0, i] + gsm[1, i] + gsm[2, i]
+    c_gsz = send(
+        *[(gsu.at[lax.rem(z + 1 + i, 4)], gsz.at[i], to) for i, to in enumerate(planes)], size=gsz
+    )
     c_zgo = collect_on(c_zgo, t_o, z_o)
-    c_gs.landed()
-    gs1[...] = gs0[...] + gsr[0] + gsr[1] + gsr[2]
-    c_gsz = share(gs1, gsz, planes)
 
     landed(c_zgb)
     fb[...] = wide(s_b[z], zb[0], zb[1], zb[2]).astype(bf16)
@@ -634,6 +652,14 @@
     )
     di_out[:, pl.ds(pl.multiple_of(768 * q, 768), 768)] = fi[q]
 
+    c_ig = []
+    for h, rows in enumerate(halves):
+        c_dx[h].landed()
+        grad = ds1[rows, :] + wide(ro[6, rows, :], ro[7, rows, :], ro[8, rows, :])
+        igs[rows, :] = grad.astype(bf16)
+        c_ig.append(swap(igs.at[rows, :], igr.at[rows, :], partner, alone))
+
+
     col_final(c_zga, s_a, za, fa)
     la[q] = fa[q]
     c_fa = to_mates(fa, la)
@@ -642,15 +668,7 @@
     do_out[...] = wide(t_o[z], z_o[0], z_o[1], z_o[2])
 
     c_gsz.landed()
-    gs2[...] = gs1[...] + gsz[0] + gsz[1] + gsz[2]
-    c_gss = send((gs2, gss, sibling))
-    c_gss.landed()
-    whole = gs2[...] + gss[...]
-    sm_out[0:8, :] = pltpu.roll(whole, lax.rem(768 - 24 * r, 768), 1)[:8, :128]
-    mine = jnp.sum(jnp.where(row == 8 + r // 8, whole, 0.0), axis=0, keepdims=True)
-    mine = pltpu.roll(jnp.broadcast_to(mine, (8, 768)), lax.rem(768 - 96 * (r % 8), 768), 1)
-    row3 = lax.broadcasted_iota(jnp.int32, (8, 128), 0)
-    sm_out[8:16, :] = jnp.where(row3 < 4, mine[:, :128], whole[8:16, :128])
+    sm_out[...] = gsu[z] + gsz[0] + gsz[1] + gsz[2]
 
     c_lo.landed()
     c_fb.landed()
@@ -703,8 +721,7 @@
     scratch = [
         v(128, 768), v(128, 768), v(4, 128, 768), v(4, 24, 576), v(4, 24, 576), v(4, 24, 768),
         v(96, 768), v(768, 576), v(768, 768), v(768, 768), v(32, 24, 768), v(768, 768),
-        v(16, 768, t=f32),
-        v(16, 768), v(3, 16, 768), v(16, 768), v(3, 16, 768), v(16, 768), v(16, 768),
+        v(16, 128, t=f32), v(32, 16, 128),
         v(16, 768, t=f32),
         v(512, 192), v(2, 512, 384), v(3072, 512), v(192, 512, t=f32), v(8, 512, t=f32),
         v(4, 192, 128), v(4, 192, 128), v(12, 128, 768), v(9, 128, 768),
@@ -721,8 +738,9 @@
         v(96, 768),
         v(32, 24, 768), v(16, 24, 768), v(16, 24, 768), v(3, 4, 24, 768), v(4, 24, 768),
         v(4, 24, 768),
-        v(128, 768), v(128, 768), v(16, 768, t=f32), v(3, 16, 768, t=f32),
-        v(16, 768, t=f32), v(3, 16, 768, t=f32), v(16, 768, t=f32), v(16, 768, t=f32),
+        v(128, 768), v(128, 768), v(16, 768, t=f32), v(32, 16, 128, t=f32),
+        v(16, 16, 128, t=f32), v(16, 16, 128, t=f32), v(3, 4, 16, 128, t=f32),
+        v(4, 16, 128, t=f32), v(3, 16, 128, t=f32),
         pltpu.SemaphoreType.DMA((COPIES,)), pltpu.SemaphoreType.DMA((COPIES,)),
     ]
     parts = pl.pallas_call(

time: 144 us -> 139 us (0.965)
  Pallas kernels: 142 us -> 136 us
    pallas_call x1, Pallas kernels: 140 us -> 133 us  [fused(): pl.pallas_call(layer_kernel, out_shape=(s(128, 768, t=bf16), s(128, 768,...]
where the time goes in v3:
time: 139 us; the launch traced here: 137 us
  Pallas kernels  136 us (98%)
    pallas_call x1, Pallas kernels, fused(): pl.pallas_call(layer_kernel, out_shape=(s(128, 768, t=bf16), s(128, 768,...  133 us

profile of v3, /device:TPU:1, one launch (start us, length us, event | category | flops | bytes accessed | tf_op | source)
XLA Modules:
  0.0 136.8 jit_solution(16201762033916959254)
XLA Ops:
  0.7 133.5 %layer.1 = (bf16[128,768]{1,0:T(8,128)(2,1)}, bf16[128,768]{1,0:T(8,128)(2,1)}, bf16[4,24,576]{2,1,0:T(8,128)(2,1)}, f32[24,768]{1,0:T(8,128)}, bf16[24,3072]{1,...) custom-call(bf16[128,768]{1,0:T(8,128)(2,1)} %tok.1, bf16[128,768]{1,0:T(8,128)(2,1)} %cot.1, ...), custom_call_target="tpu_custom_call" | custom-call | tf_op jit(solution)/shard_map/layer/pallas_call | solution.py:746
  134.1 2.5 %finish.1 = (bf16[128,768]{1,0:T(8,128)(2,1)}, f32[128,768]{1,0:T(8,128)}, f32[24,768]{1,0:T(8,128)}, f32[24,768]{1,0:T(8,128)}, f32[24,768]{1,0:T(8,128)}, /*in...) custom-call(bf16[128,768]{1,0:T(8,128)(2,1)} %get-tuple-element.43.l, ...), custom_call_target="tpu_custom_call" | custom-call | tf_op jit(solution)/shard_map/finish/pallas_call | solution.py:764

commit v4 on v3

--- a/solution.py
+++ b/solution.py
@@ -12,7 +12,7 @@
 bf16 = jnp.bfloat16
 DH = 64
 epsilon = 1e-12
-COPIES = 84
+COPIES = 90
 
 
 def dot(a, b, ca=1, cb=0):
@@ -83,7 +83,7 @@
     lo_out, igr, la, do_out, di_out, db_out, sm_out,
     xr, cr, xg, pa, sa, si, sb, wa_f, wi_f, wb_f, wo_b, wo_f,
     vec32, vecs, vf,
-    qs, kv, ee, mt, tot, mxs, mix, po, ro, hid, xh1, iv1, hg, gp, act, ds2, dg, dp, da, dms, dmi,
+    qs, kv, ee, mt, tot, mix, po, ro, hid, xh1, iv1, hg, gp, act, ds2, dg, dp, da, dms, dmi,
     dmt, dqt, dkv, kvr, dall, ds1,
     ga, ga_b, ra, s_a, za, fa,
     gi, gi_b, ri, s_i, zi, fi,
@@ -165,8 +165,19 @@
 
         return copy
 
-    def gather(ref):
-        return [send((ref.at[q], ref.at[q], mate(m))) for m in (1, 2, 3)]
+    def gather(part):
+        return [
+            send((part(q, h), part(q, h), mate(m))) for h, m in ((0, 1), (1, 2), (1, 1), (0, 2))
+        ]
+
+    def gather_on(copies, part):
+        copies[0].landed()
+        first = part(mate_q(1), 0)
+        over_y = send((first, first, mate(2)))
+        copies[1].landed()
+        second = part(mate_q(2), 1)
+        over_x = send((second, second, mate(1)))
+        return [[copies[2]], [copies[3]], [over_y, over_x]]
 
     def to_mates(src, dst):
         return send(
@@ -292,9 +303,21 @@
     )
     c_sa.landed()
     bundle(sa, wa_f)
-    c_za = spread_all(rows_a, size_a)
+    c_za = spread(rows_a, size_a)
     c_vm.landed()
     c_vs = send((vecs.at[core_slots], vecs.at[core_slots], sibling))
+
+    def part_x(j, h):
+        return xg.at[j, halves[h], :]
+
+    c_xg = []
+    for h, order in ((0, (1, 2)), (1, (2, 1))):
+        c_tok[h].landed()
+        xg[q, halves[h], :] = xr[halves[h], :]
+        c_xg += [send((part_x(q, h), part_x(q, h), mate(m))) for m in order]
+    c_xg = [c_xg[0], c_xg[2], c_xg[3], c_xg[1]]
+
+    c_za = spread_on(c_za, rows_a, size_a)
     wo_b[slot] = wo[...]
     c_zo = spread_all(rows_o, None)
     c_si.landed()
@@ -303,12 +326,6 @@
     c_sb.landed()
     wb_f[b_rows(0, z, c), :] = sb[...]
     c_zb = spread(rows_b, None)
-    c_xg = []
-    for h, rows in enumerate(halves):
-        c_tok[h].landed()
-        xg[q, rows, :] = xr[rows, :]
-        c_xg.append([send((xg.at[q, rows, :], xg.at[q, rows, :], to)) for to in mates])
-
     c_vs.landed()
     every = [vecs[ORDER[b]].astype(f32) for b in range(32)]
     vf[0:8, :] = jnp.concatenate([part[:8, :24] for part in every], axis=1)
@@ -325,6 +342,7 @@
         [turned[0:1, :192], jnp.zeros((1, 192), f32), turned[1:2, :192]], axis=1
     )
     b_in = jnp.sum(jnp.where(row == 8 + q, vf[...], 0.0), axis=0, keepdims=True)
+    c_xg = gather_on(c_xg, part_x)
     landed(c_za)
     c_ca = send(
         *[(wa_f.at[core_rows(b, c), :], wa_f.at[core_rows(b, c), :], sibling) for b in range(2)],
@@ -342,8 +360,7 @@
     for m in range(4):
         j = mate_q(m)
         if m:
-            for copies in c_xg:
-                copies[m - 1].landed()
+            landed(c_xg[m - 1])
         out = dot(xg[j], wa_f[...]) + b_qkv
         rows = pl.ds(pl.multiple_of(128 * j, 128), 128)
         qs[rows, :] = (out[:, :192].astype(bf16).astype(f32) * 0.125).astype(bf16)
@@ -380,37 +397,41 @@
     for h in range(3):
         part = slice(64 * h, 64 * h + 64)
         mt[part, :] = mt[part, :] / tot[h:h + 1, :]
-    for j in range(4):
-        mxs[j] = mt[:, 128 * j:128 * j + 128].astype(bf16)
-    mix[q] = mxs[q]
-    c_mix = to_mates(mxs, mix)
+    mix[q] = mt[...].astype(bf16)
+
+    def part_m(j, h):
+        return mix.at[j, pl.ds(96 * h, 96), :]
+
+    c_mix = gather(part_m)
     c_zi = spread_on(c_zi, rows_i, size_i)
+    c_mix = gather_on(c_mix, part_m)
 
     c_co.landed()
     for b in range(32):
         wo_f[24 * b:24 * b + 24, :] = wo_b[ORDER[b]]
-    c_mix.landed()
-    mixed = mix[...].reshape(768, 128)
-    attn = dot(mixed, wo_f[...], 0, 0) + b_out
-    x32 = xr[...].astype(f32)
-    stream = x32 + attn
-    squares_x = jnp.sum(x32 * x32)
-    squares_s = jnp.sum(stream * stream)
-    scaled, inverse = norm_parts(stream)
-    xh1[...] = scaled
-    iv1[...] = jnp.broadcast_to(inverse, iv1.shape)
-    hidden = scaled * gain1 + shift1
-    hid[...] = hidden
-    hg[q] = hidden.astype(bf16)
-    c_hg = gather(hg)
     c_zb = spread_on(c_zb, rows_b, None)
-    c_cot = swap(cot, cr, partner, alone)
-
     landed(c_zi)
     c_ci = send(
         *[(wi_f.at[core_rows(b, c), :], wi_f.at[core_rows(b, c), :], sibling) for b in range(2)],
         size=wi_f.at[pl.ds(0, 384), :],
     )
+    for copies in c_mix:
+        landed(copies)
+    c_cot = swap(cot, cr, partner, alone)
+    squares_x = squares_s = 0.0
+    for j in range(4):
+        mixed = mix[:, :, 128 * j:128 * j + 128].reshape(768, 128)
+        x32 = xg[j].astype(f32)
+        stream = x32 + dot(mixed, wo_f[...], 0, 0) + b_out
+        squares_x += jnp.where(q == j, jnp.sum(x32 * x32), 0.0)
+        squares_s += jnp.where(q == j, jnp.sum(stream * stream), 0.0)
+        scaled, inverse = norm_parts(stream)
+        xh1[j] = scaled
+        iv1[j] = jnp.broadcast_to(inverse, (128, 128))
+        hidden = scaled * gain1 + shift1
+        hid[j] = hidden
+        hg[j] = hidden.astype(bf16)
+
     landed(c_zb)
     c_cb = send(
         *[(wb_f.at[b_rows(0, zz, c), :], wb_f.at[b_rows(0, zz, c), :], sibling) for zz in range(4)],
@@ -427,19 +448,19 @@
     def ffn_out(j):
         return dot(act[j], wb_f[...])
 
-    ffn(q)
-    c_cb.landed()
-    own_part = ffn_out(q)
     c_ffn = []
     for m in (1, 2, 3):
-        c_hg[m - 1].landed()
         j = mate_q(m)
         ffn(j)
+        if m == 1:
+            c_cb.landed()
         po[j] = ffn_out(j).astype(bf16)
         c_ffn.append(send((po.at[j], ro.at[m - 1], mate(m))))
+    ffn(q)
+    own_part = ffn_out(q)
     landed(c_ffn)
     out = own_part + b_back + wide(ro[0], ro[1], ro[2])
-    scaled2, inverse2 = norm_parts(hid[...] + out)
+    scaled2, inverse2 = norm_parts(hid[q] + out)
     los[...] = (scaled2 * gain2 + shift2).astype(bf16)
     c_cot.landed()
     dy = cr[...].astype(f32)
@@ -450,7 +471,11 @@
     low = dsum2.astype(bf16)
     dg[q] = low
     back_grad = jnp.sum(low.astype(f32), axis=0, keepdims=True)
-    c_dg = gather(dg)
+
+    def part_g(j, h):
+        return dg.at[j, halves[h], :]
+
+    c_dg = gather(part_g)
     c_lo = swap(los, lo_out, partner, alone)
 
     def ffn_back(j):
@@ -459,9 +484,10 @@
         return dot(dp[j], wi_f[...], 1, 1)
 
     own_part = ffn_back(q)
+    c_dg = gather_on(c_dg, part_g)
     c_dh = []
     for m in (1, 2, 3):
-        c_dg[m - 1].landed()
+        landed(c_dg[m - 1])
         j = mate_q(m)
         po[4 + j] = ffn_back(j).astype(bf16)
         c_dh.append(send((po.at[4 + j], ro.at[2 + m], mate(m))))
@@ -505,9 +531,9 @@
 
     landed(c_dh)
     dhidden = ds2[...] + own_part + wide(ro[3], ro[4], ro[5])
-    gain1_grad = jnp.sum(dhidden * xh1[...], axis=0, keepdims=True)
+    gain1_grad = jnp.sum(dhidden * xh1[q], axis=0, keepdims=True)
     shift1_grad = jnp.sum(dhidden, axis=0, keepdims=True)
-    dsum1 = norm_back(dhidden, xh1[...], iv1[:, :1], gain1)
+    dsum1 = norm_back(dhidden, xh1[q], iv1[q][:, :1], gain1)
     ds1[...] = dsum1
     low = dsum1.astype(bf16)
     da[...] = low
@@ -519,7 +545,8 @@
     c_dm = to_mates(dms, dmi)
     c_zgb = collect_on(c_zgb, s_b, zb)
 
-    part = dot(mix[...].reshape(768, 128), da[...])
+    own_cols = pl.ds(pl.multiple_of(128 * q, 128), 128)
+    part = dot(mix[:, :, own_cols].reshape(768, 128), da[...])
     for b in range(32):
         go_b[ORDER[b]] = part[24 * b:24 * b + 24].astype(bf16)
     other_o = pl.ds(pl.multiple_of(16 * (1 - c), 16), 16)
@@ -724,8 +751,8 @@
         v(16, 128, t=f32), v(32, 16, 128),
         v(16, 768, t=f32),
         v(512, 192), v(2, 512, 384), v(3072, 512), v(192, 512, t=f32), v(8, 512, t=f32),
-        v(4, 192, 128), v(4, 192, 128), v(12, 128, 768), v(9, 128, 768),
-        v(128, 768, t=f32), v(128, 768, t=f32), v(128, 128, t=f32), v(4, 128, 768),
+        v(4, 192, 512), v(12, 128, 768), v(9, 128, 768),
+        v(4, 128, 768, t=f32), v(4, 128, 768, t=f32), v(4, 128, 128, t=f32), v(4, 128, 768),
         v(4, 128, 768, t=f32), v(4, 128, 768), v(128, 768, t=f32), v(4, 128, 768),
         v(4, 128, 768), v(128, 768), v(4, 192, 128), v(4, 192, 128),
         v(192, 512, t=f32), v(192, 512, t=f32), v(2, 512, 384, t=f32), v(512, 384, t=f32),

time: 139 us -> 128 us (0.921)
  Pallas kernels: 136 us -> 126 us
    pallas_call x1, Pallas kernels: 133 us -> 123 us  [fused(): pl.pallas_call(layer_kernel, out_shape=(s(128, 768, t=bf16), s(128, 768,...]
where the time goes in v4:
time: 128 us; the launch traced here: 127 us
  Pallas kernels  126 us (98%)
    pallas_call x1, Pallas kernels, fused(): pl.pallas_call(layer_kernel, out_shape=(s(128, 768, t=bf16), s(128, 768,...  123 us

profile of v4, /device:TPU:1, one launch (start us, length us, event | category | flops | bytes accessed | tf_op | source)
XLA Modules:
  0.0 126.6 jit_solution(10335961611720368828)
XLA Ops:
  0.7 123.3 %layer.1 = (bf16[128,768]{1,0:T(8,128)(2,1)}, bf16[128,768]{1,0:T(8,128)(2,1)}, bf16[4,24,576]{2,1,0:T(8,128)(2,1)}, f32[24,768]{1,0:T(8,128)}, bf16[24,3072]{1,...) custom-call(bf16[128,768]{1,0:T(8,128)(2,1)} %tok.1, bf16[128,768]{1,0:T(8,128)(2,1)} %cot.1, ...), custom_call_target="tpu_custom_call" | custom-call | tf_op jit(solution)/shard_map/layer/pallas_call | solution.py:773
  124.0 2.5 %finish.1 = (bf16[128,768]{1,0:T(8,128)(2,1)}, f32[128,768]{1,0:T(8,128)}, f32[24,768]{1,0:T(8,128)}, f32[24,768]{1,0:T(8,128)}, f32[24,768]{1,0:T(8,128)}, /*in...) custom-call(bf16[128,768]{1,0:T(8,128)(2,1)} %get-tuple-element.43.l, ...), custom_call_target="tpu_custom_call" | custom-call | tf_op jit(solution)/shard_map/finish/pallas_call | solution.py:791

commit v5 on v4

--- a/solution.py
+++ b/solution.py
@@ -12,7 +12,7 @@
 bf16 = jnp.bfloat16
 DH = 64
 epsilon = 1e-12
-COPIES = 90
+COPIES = 93
 
 
 def dot(a, b, ca=1, cb=0):
@@ -83,8 +83,8 @@
     lo_out, igr, la, do_out, di_out, db_out, sm_out,
     xr, cr, xg, pa, sa, si, sb, wa_f, wi_f, wb_f, wo_b, wo_f,
     vec32, vecs, vf,
-    qs, kv, ee, mt, tot, mix, po, ro, hid, xh1, iv1, hg, gp, act, ds2, dg, dp, da, dms, dmi,
-    dmt, dqt, dkv, kvr, dall, ds1,
+    qs, kv, ee, mt, tot, mix, po, pf, rd, ro, hid, xh1, iv1, hg, gp, act, ds2, dg, dp, da, dms, dmi,
+    dmt, dqt, dkv, kvs, kvr, dall, ds1,
     ga, ga_b, ra, s_a, za, fa,
     gi, gi_b, ri, s_i, zi, fi,
     gb, gb_b, rb, s_b, zb, fb,
@@ -448,18 +448,33 @@
     def ffn_out(j):
         return dot(act[j], wb_f[...])
 
-    c_ffn = []
-    for m in (1, 2, 3):
-        j = mate_q(m)
-        ffn(j)
-        if m == 1:
-            c_cb.landed()
-        po[j] = ffn_out(j).astype(bf16)
-        c_ffn.append(send((po.at[j], ro.at[m - 1], mate(m))))
+    low_half, high_half = halves
+    over_x, over_y, across = mate_q(1), mate_q(2), mate_q(3)
+    ffn(across)
+    c_cb.landed()
+    po[across] = ffn_out(across).astype(bf16)
+    c_far = [
+        send((po.at[across, low_half, :], rd.at[0], mate(1))),
+        send((po.at[across, high_half, :], rd.at[1], mate(2))),
+    ]
+    ffn(over_x)
+    pf[0] = ffn_out(over_x)
+    po[over_x, low_half, :] = pf[0, low_half, :].astype(bf16)
+    c_ffn = [send((po.at[over_x, low_half, :], ro.at[0, low_half, :], mate(1)))]
+    ffn(over_y)
+    pf[1] = ffn_out(over_y)
+    po[over_y, high_half, :] = pf[1, high_half, :].astype(bf16)
+    c_ffn.append(send((po.at[over_y, high_half, :], ro.at[1, high_half, :], mate(2))))
+    c_far[1].landed()
+    po[over_x, high_half, :] = wide(pf[0, high_half, :], rd[1]).astype(bf16)
+    c_ffn.append(send((po.at[over_x, high_half, :], ro.at[0, high_half, :], mate(1))))
+    c_far[0].landed()
+    po[over_y, low_half, :] = wide(pf[1, low_half, :], rd[0]).astype(bf16)
+    c_ffn.append(send((po.at[over_y, low_half, :], ro.at[1, low_half, :], mate(2))))
     ffn(q)
     own_part = ffn_out(q)
     landed(c_ffn)
-    out = own_part + b_back + wide(ro[0], ro[1], ro[2])
+    out = own_part + b_back + wide(ro[0], ro[1])
     scaled2, inverse2 = norm_parts(hid[q] + out)
     los[...] = (scaled2 * gain2 + shift2).astype(bf16)
     c_cot.landed()
@@ -552,6 +567,12 @@
     other_o = pl.ds(pl.multiple_of(16 * (1 - c), 16), 16)
     c_rgo = send((go_b.at[other_o], r_o, sibling))
 
+    c_rgo.landed()
+    for i in range(16):
+        s_o[i] = wide(go_b[16 * c + i], r_o[i]).astype(bf16)
+    c_pgo = send(
+        *[(s_o.at[pl.ds(4 * mate_q(m), 4)], p_o.at[m - 1], mate(m)) for m in (1, 2, 3)], size=p_o
+    )
     c_dm.landed()
     for j in range(4):
         dmt[:, 128 * j:128 * j + 128] = dmi[j].astype(f32)
@@ -581,18 +602,13 @@
 
     backward_chunk(1 - c, 1, 0)
     backward_chunk(1 - c, 1, 1)
-    c_dkv = send((dkv.at[1 - c], kvr, sibling))
-    c_rgo.landed()
-    for i in range(16):
-        s_o[i] = wide(go_b[16 * c + i], r_o[i]).astype(bf16)
-    c_pgo = send(
-        *[(s_o.at[pl.ds(4 * mate_q(m), 4)], p_o.at[m - 1], mate(m)) for m in (1, 2, 3)], size=p_o
-    )
+    kvs[...] = dkv[1 - c].astype(bf16)
+    c_dkv = send((kvs, kvr, sibling))
     backward_chunk(c, 0, 0)
     backward_chunk(c, 0, 1)
     dall[:, :192] = jnp.transpose(dqt[...] * 0.125).astype(bf16)
     c_dkv.landed()
-    dall[:, 192:] = (dkv[c] + kvr[...]).astype(bf16)
+    dall[:, 192:] = wide(dkv[c], kvr[...]).astype(bf16)
 
     sums = jnp.sum(dall[...].astype(f32), axis=0, keepdims=True)
     rest = jnp.zeros((1, 576), f32)
@@ -751,11 +767,11 @@
         v(16, 128, t=f32), v(32, 16, 128),
         v(16, 768, t=f32),
         v(512, 192), v(2, 512, 384), v(3072, 512), v(192, 512, t=f32), v(8, 512, t=f32),
-        v(4, 192, 512), v(12, 128, 768), v(9, 128, 768),
+        v(4, 192, 512), v(12, 128, 768), v(2, 128, 768, t=f32), v(2, 64, 768), v(9, 128, 768),
         v(4, 128, 768, t=f32), v(4, 128, 768, t=f32), v(4, 128, 128, t=f32), v(4, 128, 768),
         v(4, 128, 768, t=f32), v(4, 128, 768), v(128, 768, t=f32), v(4, 128, 768),
         v(4, 128, 768), v(128, 768), v(4, 192, 128), v(4, 192, 128),
-        v(192, 512, t=f32), v(192, 512, t=f32), v(2, 512, 384, t=f32), v(512, 384, t=f32),
+        v(192, 512, t=f32), v(192, 512, t=f32), v(2, 512, 384, t=f32), v(512, 384), v(512, 384),
         v(512, 576), v(128, 768, t=f32),
         v(768, 576, t=f32), v(768, 576), v(2, 192, 576), v(4, 96, 576), v(4, 96, 576),
         v(4, 24, 576),

time: 128 us -> 125 us (0.977)
  Pallas kernels: 126 us -> 124 us
    pallas_call x1, Pallas kernels: 123 us -> 121 us  [fused(): pl.pallas_call(layer_kernel, out_shape=(s(128, 768, t=bf16), s(128, 768,...]
where the time goes in v5:
time: 125 us
  Pallas kernels  124 us (99%)
    pallas_call x1, Pallas kernels, fused(): pl.pallas_call(layer_kernel, out_shape=(s(128, 768, t=bf16), s(128, 768,...  121 us

profile of v5, /device:TPU:1, one launch (start us, length us, event | category | flops | bytes accessed | tf_op | source)
XLA Modules:
  0.0 124.6 jit_solution(7268589362480533068)
XLA Ops:
  0.7 121.3 %layer.1 = (bf16[128,768]{1,0:T(8,128)(2,1)}, bf16[128,768]{1,0:T(8,128)(2,1)}, bf16[4,24,576]{2,1,0:T(8,128)(2,1)}, f32[24,768]{1,0:T(8,128)}, bf16[24,3072]{1,...) custom-call(bf16[128,768]{1,0:T(8,128)(2,1)} %tok.1, bf16[128,768]{1,0:T(8,128)(2,1)} %cot.1, ...), custom_call_target="tpu_custom_call" | custom-call | tf_op jit(solution)/shard_map/layer/pallas_call | solution.py:789
  122.0 2.5 %finish.1 = (bf16[128,768]{1,0:T(8,128)(2,1)}, f32[128,768]{1,0:T(8,128)}, f32[24,768]{1,0:T(8,128)}, f32[24,768]{1,0:T(8,128)}, f32[24,768]{1,0:T(8,128)}, /*in...) custom-call(bf16[128,768]{1,0:T(8,128)(2,1)} %get-tuple-element.43.l, ...), custom_call_target="tpu_custom_call" | custom-call | tf_op jit(solution)/shard_map/finish/pallas_call | solution.py:807
